TPU v7x, 32 devices: a whole 2x2x4 slice. The times are simulated.
32 devices in a mesh: blk: 16 (over z, y, x), grp: 2 (over core).
Axes of the slice: x: 2, y: 2, z: 4, core: 2. Of those that a mesh axis runs over, the one named last changes fastest.
Arguments:
- excitation: bfloat16 [32, 1024, 256], P('blk'), may hold values from -6 to 6
- inverse_self: bfloat16 [32, 1024, 1024], P('blk', 'grp'), may hold values from -0.1875 to 0.1875
- coupling: bfloat16 [32, 4, 1024, 1024], P('blk', None, 'grp'), may hold values from -0.1875 to 0.1875
- neighbour_mask: int32 [32, 4], P('blk'), may hold values 0 or 1
- sketch: float32 [5, 256, 32], replicated, may hold values from -6 to 6
Outputs:
- bases: float32 [32, 1024, 32], P('blk', 'grp')
- reduced_coupling: float32 [32, 4, 32, 32], P('blk')
- reduced_excitation: float32 [32, 32, 256], P('blk')
Inputs may be any that keep to these rules, and one draw needn't show every extreme that they name: `neighbour_mask`: 1 where the block at that slot's offset adds secondary currents, 0 where it does not; slots pointing outside the array add nothing in any case.
All inputs are finite; a program needn't handle non-finite values.
Results may differ from a plain program's by a relative error of at most 0.0003.
Values sent between devices are 32-bit elements; how exact they have to be, the bound alone decides.
A program may use at most 64 MiB of HBM per device.

v0:
```python
import math

import jax
import jax.numpy as jnp
from jax import lax
from jax.sharding import PartitionSpec as P

neighbour_offsets = (-2, -1, 1, 2)


def extended(array, sides, width):
    for axis, dim in sides:
        size, length = (lax.axis_size(axis), array.shape[dim])
        up = [(i, (i + 1) % size) for i in range(size - 1)]
        down = [(j, i) for i, j in up]
        last = lax.slice_in_dim(array, length - width, length, axis=dim)
        initial = lax.slice_in_dim(array, 0, width, axis=dim)
        before = lax.ppermute(last, axis, up)
        after = lax.ppermute(initial, axis, down)
        array = jnp.concatenate([before, array, after], axis=dim)
    return array


def exact_einsum(form, left, right):
    return jnp.einsum(
        form, left, right, precision=lax.Precision.HIGHEST, preferred_element_type=jnp.float32
    )


def shards(excitation, inverse_self, coupling, neighbour_mask, sketch):
    blocks, unknowns, columns = excitation.shape
    shard_rows = inverse_self.shape[1]
    retained = sketch.shape[2]
    slots = coupling.shape[1]
    row_start = lax.axis_index("grp") * shard_rows
    own_excitation = lax.dynamic_slice_in_dim(excitation, row_start, shard_rows, 1)
    primary = jnp.einsum(
        "bnm,bmp->bnp", inverse_self, excitation, preferred_element_type=jnp.float32
    )
    weights_mask = neighbour_mask.astype(jnp.float32)
    outgoing = exact_einsum("bnp,kpr->bnkr", primary, sketch[1:])
    outgoing = outgoing.reshape(blocks, shard_rows, slots * retained)
    own_whole = lax.all_gather(outgoing, "grp", axis=1, tiled=True)
    nearby = extended(own_whole, (("blk", 0),), 2)
    sources = jnp.zeros((blocks, shard_rows, retained), jnp.float32)
    for slot_index, offset in enumerate(neighbour_offsets):
        neighbour = nearby[2 + offset : 2 + offset + blocks]
        sketch_piece = neighbour[:, :, slot_index * retained : (slot_index + 1) * retained]
        coupled_term = exact_einsum("bnm,bmr->bnr", coupling[:, slot_index], sketch_piece)
        sources = sources + weights_mask[:, slot_index, None, None] * coupled_term
    all_sources = lax.all_gather(sources, "grp", axis=1, tiled=True)
    sketched = exact_einsum("bnp,pr->bnr", primary, sketch[0]) - exact_einsum(
        "bnm,bmr->bnr", inverse_self, all_sources
    )
    gram_part = exact_einsum("bnr,bns->brs", sketched, sketched)
    gram_total = lax.psum(gram_part, "grp") / unknowns
    chol_lower = jnp.linalg.cholesky(gram_total)
    bases = lax.linalg.triangular_solve(
        chol_lower, sketched, left_side=False, lower=True, transpose_a=True
    )
    basis_shards = extended(bases, (("blk", 0),), 2)
    basis_near = lax.all_gather(basis_shards, "grp", axis=1, tiled=True)
    stacked = []
    for slot_index, offset in enumerate(neighbour_offsets):
        coupled_basis = exact_einsum(
            "bnm,bmr->bnr", coupling[:, slot_index], basis_near[2 + offset : 2 + offset + blocks]
        )
        stacked.append(exact_einsum("bnr,bns->brs", bases, coupled_basis))
    coupled_part = jnp.stack(stacked, axis=1)
    driven_part = exact_einsum("bnr,bnp->brp", bases, own_excitation)
    coupled_sum, driven_sum = lax.psum((coupled_part, driven_part), "grp")
    norm_scale = 1.0 / math.sqrt(unknowns)
    return (bases, coupled_sum * norm_scale, driven_sum * norm_scale)


def solution(mesh):
    return jax.shard_map(
        shards,
        mesh=mesh,
        in_specs=(
            P("blk", None, None),
            P("blk", "grp", None),
            P("blk", None, "grp", None),
            P("blk", None),
            P(),
        ),
        out_specs=(P("blk", "grp", None), P("blk", None, None, None), P("blk", None, None)),
        check_vma=False,
    )
```

profile of v0, /device:TPU:17, one launch (start us, length us, event | category | flops | bytes accessed | tf_op | source)
XLA Modules:
  0.0 157.2 jit_solution(13111443732232478313)
XLA Ops:
  8.8 1.9 %fusion.68 = f32[2,512,256]{2,1,0:T(8,128)S(1)} fusion(bf16[2,512,1024]{2,1,0:T(8,128)(2,1)S(1)} %copy-done, bf16[2,1024,256]{2,1,0:T(8,128)(2,1)} %param.5), kind=kOutput, calls=%fused_computation.74 | convolution fusion | flops 536870912 | bytes 4194304 | tf_op jit(solution)/shard_map/bnm,bmp->bnp/dot_general | solution.py:37
  10.7 2.0 %fusion.49 = f32[2,512,4,32]{1,3,2,0:T(8,128)} fusion(f32[2,512,256]{2,1,0:T(8,128)S(1)} %fusion.68, f32[5,256,32]{1,2,0:T(8,128)S(1)} %copy-done.4), kind=kOutput, calls=%fused_computation.38 | convolution fusion | flops 402653184 | bytes 1703936 | tf_op jit(solution)/shard_map/bnp,kpr->bnkr/dot_general | solution.py:25
  12.8 10.9 %all-gather.2.cloned.1.call-done = f32[2,1024,128]{1,2,0:T(8,128)} async-done(((f32[2,512,128]{1,2,0:T(8,128)}), f32[2,1024,128]{1,2,0:T(8,128)}) %all-gather.2.cloned.1.call-update) | async-done | bytes 1048592 | tf_op jit(solution)/shard_map/all_gather | solution.py:43
  23.8 4.0 %collective-permute-start.1 = (f32[2,1024,128]{1,2,0:T(8,128)}, f32[2,1024,128]{1,2,0:T(8,128)}, u32[]{:S(2)}, u32[]{:S(2)}) collective-permute-start(f32[2,1024,128]{1,2,0:T(8,128)} %all-gather.2.cloned.1.call-done), channel_id=1, source_target_pairs={{2,0},{4,2},{6,4},{8,6},{10,8},{12,10},{14,12},{16,14},{18,16},{20... | collective-permute-start | bytes 3145736 | tf_op jit(solution)/shard_map/ppermute | solution.py:19
  27.7 1.9 %collective-permute-start = (f32[2,1024,128]{1,2,0:T(8,128)}, f32[2,1024,128]{1,2,0:T(8,128)}, u32[]{:S(2)}, u32[]{:S(2)}) collective-permute-start(f32[2,1024,128]{1,2,0:T(8,128)} %all-gather.2.cloned.1.call-done), channel_id=1, source_target_pairs={{0,2},{2,4},{4,6},{6,8},{8,10},{10,12},{12,14},{14,16},{16,18},{18... | collective-permute-start | bytes 3145736 | tf_op jit(solution)/shard_map/ppermute | solution.py:18
  31.0 19.5 %collective-permute-done.1 = f32[2,1024,128]{1,2,0:T(8,128)} collective-permute-done((f32[2,1024,128]{1,2,0:T(8,128)}, f32[2,1024,128]{1,2,0:T(8,128)}, u32[]{:S(2)}, u32[]{:S(2)}) %collective-permute-start.1) | collective-permute-done | bytes 1048608 | tf_op jit(solution)/shard_map/ppermute | solution.py:19
  50.5 3.7 %fusion.42 = f32[2,32,512]{2,1,0:T(8,128)S(1)} fusion(bf16[2,4,512,1024]{3,2,1,0:T(8,128)(2,1)} %param.7, f32[2,1024,128]{1,2,0:T(8,128)} %collective-permute-done.1, f32[2,1024,128]{1,2,0:T(8,128)} %all-gather.2.cloned.1.call-done, f32[2]{0:T(128)S(1)} %get-tuple-element.11), kind=kOutput, calls=%fused_computation.30 | convolution fusion | flops 402751488 | bytes 4325384 | tf_op jit(solution)/shard_map/bnm,bmr->bnr/dot_general | solution.py:25
  54.2 3.7 %fusion.45 = f32[2,32,512]{2,1,0:T(8,128)S(1)} fusion(bf16[2,4,512,1024]{3,2,1,0:T(8,128)(2,1)} %param.7, f32[2,1024,128]{1,2,0:T(8,128)} %collective-permute-done.1, f32[2]{0:T(128)S(1)} %get-tuple-element.10), kind=kOutput, calls=%fused_computation.31 | convolution fusion | flops 402685952 | bytes 2490376 | tf_op jit(solution)/shard_map/bnm,bmr->bnr/dot_general | solution.py:25
  57.9 16.5 %collective-permute-done = f32[2,1024,128]{1,2,0:T(8,128)} collective-permute-done((f32[2,1024,128]{1,2,0:T(8,128)}, f32[2,1024,128]{1,2,0:T(8,128)}, u32[]{:S(2)}, u32[]{:S(2)}) %collective-permute-start) | collective-permute-done | bytes 1048608 | tf_op jit(solution)/shard_map/ppermute | solution.py:18
  74.3 3.6 %fusion.39 = f32[2,32,512]{2,1,0:T(8,128)S(1)} fusion(bf16[2,4,512,1024]{3,2,1,0:T(8,128)(2,1)} %param.7, f32[2,1024,128]{1,2,0:T(8,128)S(1)} %copy-done.2, f32[2,1024,128]{1,2,0:T(8,128)} %collective-permute-done, f32[2]{0:T(128)S(1)} %get-tuple-element.12), kind=kOutput, calls=%fused_computation.29 | convolution fusion | flops 402751488 | bytes 4325384 | tf_op jit(solution)/shard_map/bnm,bmr->bnr/dot_general | solution.py:25
  77.9 3.6 %fusion.36 = f32[2,512,32]{1,2,0:T(8,128)S(1)} fusion(f32[2,32,512]{2,1,0:T(8,128)S(1)} %fusion.45, f32[2,32,512]{2,1,0:T(8,128)S(1)} %fusion.42, f32[2,32,512]{2,1,0:T(8,128)S(1)} %fusion.39, bf16[2,4,512,1024]{3,2,1,0:T(8,128)(2,1)} %param.7, f32[2,1024,128]{1,2,0:T(8,128)} %collective-permute-done, f32[2]{0:T(128)S(1)} %get-tuple-element.9), kind=kOutput, calls=%fused_computation.28 | convolution fusion | flops 402784256 | bytes 2883592 | tf_op jit(solution)/shard_map/bnm,bmr->bnr/dot_general | solution.py:25
  81.6 2.2 %all_gather.10 = f32[2,1024,32]{1,2,0:T(8,128)S(1)} all-gather(f32[2,512,32]{1,2,0:T(8,128)S(1)} %fusion.36), channel_id=1, replica_groups=mesh['blk'=16,'grp'=2] {'grp'}, dimensions={1}, use_global_device_ids=true | all-gather | bytes 393216 | tf_op jit(solution)/shard_map/all_gather | solution.py:51
  85.9 3.6 %psum.21 = f32[2,32,32]{1,2,0:T(8,128)S(1)} all-reduce(f32[2,32,32]{1,2,0:T(8,128)S(1)} %fusion.69), channel_id=1, replica_groups=mesh['blk'=16,'grp'=2] {'grp'}, use_global_device_ids=true, to_apply=%region_0.0 | all-reduce | flops 2048 | bytes 16384 | tf_op jit(solution)/shard_map/psum | solution.py:56
  89.7 5.9 %custom-call.7 = f32[2,32,32]{2,1,0:T(8,128)S(1)} custom-call(f32[2,32,32]{2,1,0:T(8,128)S(1)} %fusion.61), custom_call_target="Cholesky" | custom-call | tf_op jit(solution)/shard_map/jit(cholesky)/cholesky | solution.py:57
  95.7 4.9 %custom-call.8 = f32[2,1,32,32]{2,3,1,0:T(8,128)S(1)} custom-call(f32[2,1,32,32]{3,2,1,0:T(8,128)S(1)} %select_bitcast_fusion), custom_call_target="InvertDiagBlocksLowerTriangular" | custom-call | tf_op jit(solution)/shard_map/triangular_solve | solution.py:58
  102.1 8.6 %collective-permute-start.3 = (f32[2,512,32]{1,2,0:T(8,128)S(1)}, f32[2,512,32]{1,2,0:T(8,128)S(1)}, u32[]{:S(2)}, u32[]{:S(2)}) collective-permute-start(f32[2,512,32]{1,2,0:T(8,128)S(1)} %fusion.59), channel_id=1, source_target_pairs={{2,0},{4,2},{6,4},{8,6},{10,8},{12,10},{14,12},{16,14},{18,16},{20... | collective-permute-start | bytes 393224 | tf_op jit(solution)/shard_map/ppermute | solution.py:19
  110.7 1.9 %collective-permute-start.2 = (f32[2,512,32]{1,2,0:T(8,128)S(1)}, f32[2,512,32]{1,2,0:T(8,128)S(1)}, u32[]{:S(2)}, u32[]{:S(2)}) collective-permute-start(f32[2,512,32]{1,2,0:T(8,128)S(1)} %fusion.59), channel_id=1, source_target_pairs={{0,2},{2,4},{4,6},{6,8},{8,10},{10,12},{12,14},{14,16},{16,18},{18... | collective-permute-start | bytes 393224 | tf_op jit(solution)/shard_map/ppermute | solution.py:18
  112.6 14.1 %all-reduce.2.cloned.1.call-done = f32[2,32,256]{2,1,0:T(8,128)} async-done(((f32[2,32,256]{2,1,0:T(8,128)}), f32[2,32,256]{2,1,0:T(8,128)}) %all-reduce.2.cloned.1.call-update) | async-done | bytes 65552 | tf_op jit(solution)/shard_map/psum | solution.py:71
  128.2 2.5 %all_gather.11 = f32[6,1024,32]{1,2,0:T(8,128)S(1)} all-gather(f32[6,512,32]{1,2,0:T(8,128)S(1)} %pad_maximum_fusion), channel_id=1, replica_groups=mesh['blk'=16,'grp'=2] {'grp'}, dimensions={1}, use_global_device_ids=true | all-gather | bytes 1179648 | tf_op jit(solution)/shard_map/all_gather | solution.py:62
  130.8 3.5 %fusion = f32[2,32,512]{2,1,0:T(8,128)S(1)} fusion(f32[6,1024,32]{1,2,0:T(8,128)S(1)} %all_gather.11, bf16[2,4,512,1024]{3,2,1,0:T(8,128)(2,1)} %param.7), kind=kOutput, calls=%fused_computation | convolution fusion | flops 402653184 | bytes 3014656 | tf_op jit(solution)/shard_map/bnm,bmr->bnr/dot_general | solution.py:25
  134.3 3.5 %fusion.4 = f32[2,32,512]{2,1,0:T(8,128)S(1)} fusion(f32[6,1024,32]{1,2,0:T(8,128)S(1)} %all_gather.11, bf16[2,4,512,1024]{3,2,1,0:T(8,128)(2,1)} %param.7), kind=kOutput, calls=%fused_computation.4 | convolution fusion | flops 402653184 | bytes 3014656 | tf_op jit(solution)/shard_map/bnm,bmr->bnr/dot_general | solution.py:25
  137.8 3.5 %fusion.8 = f32[2,32,512]{2,1,0:T(8,128)S(1)} fusion(f32[6,1024,32]{1,2,0:T(8,128)S(1)} %all_gather.11, bf16[2,4,512,1024]{3,2,1,0:T(8,128)(2,1)} %param.7), kind=kOutput, calls=%fused_computation.8 | convolution fusion | flops 402653184 | bytes 3014656 | tf_op jit(solution)/shard_map/bnm,bmr->bnr/dot_general | solution.py:25
  141.3 3.5 %fusion.12 = f32[2,32,512]{2,1,0:T(8,128)S(1)} fusion(f32[6,1024,32]{1,2,0:T(8,128)S(1)} %all_gather.11, bf16[2,4,512,1024]{3,2,1,0:T(8,128)(2,1)} %param.7), kind=kOutput, calls=%fused_computation.12 | convolution fusion | flops 402653184 | bytes 3014656 | tf_op jit(solution)/shard_map/bnm,bmr->bnr/dot_general | solution.py:25
  145.9 3.8 %psum.22 = f32[2,4,32,32]{3,2,0,1:T(8,128)S(1)} all-reduce(f32[2,4,32,32]{3,2,0,1:T(8,128)S(1)} %pad_maximum_fusion.5), channel_id=1, replica_groups=mesh['blk'=16,'grp'=2] {'grp'}, use_global_device_ids=true, to_apply=%region_3.4 | all-reduce | flops 8192 | bytes 65536 | tf_op jit(solution)/shard_map/psum | solution.py:71
  (42 shorter events, 10.0 us)
Async XLA Ops:
  7.2 1.6 %copy-start = (bf16[2,512,1024]{2,1,0:T(8,128)(2,1)S(1)}, bf16[2,512,1024]{2,1,0:T(8,128)(2,1)}, u32[]{:S(2)}) copy-start(bf16[2,512,1024]{2,1,0:T(8,128)(2,1)} %param.6) | copy-start | bytes 6291460
  7.2 3.5 %copy-start.4 = (f32[5,256,32]{1,2,0:T(8,128)S(1)}, f32[5,256,32]{1,2,0:T(8,128)}, u32[]{:S(2)}) copy-start(f32[5,256,32]{1,2,0:T(8,128)} %param.9) | copy-start | bytes 491524
  7.2 16.6 %all-gather.2.cloned.1.call-start = ((), (), s32[]{:S(2)}) async-start(), calls=%async_computation | async-start | bytes 1572864 | tf_op jit(solution)/shard_map/all_gather | solution.py:43
  10.7 19.0 %copy-start.5 = (s32[2,4]{1,0:T(2,128)S(1)}, s32[2,4]{1,0:T(2,128)}, u32[]{:S(2)}) copy-start(s32[2,4]{1,0:T(2,128)} %param.8) | copy-start | bytes 100
  12.8 114.0 %all-reduce.2.cloned.1.call-start = ((), (), s32[]{:S(2)}) async-start(), calls=%async_computation.1 | async-start | bytes 131072 | tf_op jit(solution)/shard_map/psum | solution.py:71
  23.8 26.8 %collective-permute-start.1 = (f32[2,1024,128]{1,2,0:T(8,128)}, f32[2,1024,128]{1,2,0:T(8,128)}, u32[]{:S(2)}, u32[]{:S(2)}) collective-permute-start(f32[2,1024,128]{1,2,0:T(8,128)} %all-gather.2.cloned.1.call-done), channel_id=1, source_target_pairs={{2,0},{4,2},{6,4},{8,6},{10,8},{12,10},{14,12},{16,14},{18,16},{20... | collective-permute-start | bytes 3145736 | tf_op jit(solution)/shard_map/ppermute | solution.py:19
  27.7 46.6 %collective-permute-start = (f32[2,1024,128]{1,2,0:T(8,128)}, f32[2,1024,128]{1,2,0:T(8,128)}, u32[]{:S(2)}, u32[]{:S(2)}) collective-permute-start(f32[2,1024,128]{1,2,0:T(8,128)} %all-gather.2.cloned.1.call-done), channel_id=1, source_target_pairs={{0,2},{2,4},{4,6},{6,8},{8,10},{10,12},{12,14},{14,16},{16,18},{18... | collective-permute-start | bytes 3145736 | tf_op jit(solution)/shard_map/ppermute | solution.py:18
  54.2 20.2 %copy-start.2 = (f32[2,1024,128]{1,2,0:T(8,128)S(1)}, f32[2,1024,128]{1,2,0:T(8,128)}, u32[]{:S(2)}) copy-start(f32[2,1024,128]{1,2,0:T(8,128)} %all-gather.2.cloned.1.call-done) | copy-start | bytes 3145732
  81.5 19.5 %copy-start.3 = (bf16[2,1024,256]{2,1,0:T(8,128)(2,1)S(1)}, bf16[2,1024,256]{2,1,0:T(8,128)(2,1)}, u32[]{:S(2)}) copy-start(bf16[2,1024,256]{2,1,0:T(8,128)(2,1)} %param.5) | copy-start | bytes 3145732
  101.0 44.6 %copy-start.1 = (f32[2,512,32]{1,2,0:T(8,128)}, f32[2,512,32]{1,2,0:T(8,128)S(1)}, u32[]{:S(2)}) copy-start(f32[2,512,32]{1,2,0:T(8,128)S(1)} %fusion.59) | copy-start | bytes 393220
  102.1 26.2 %collective-permute-start.3 = (f32[2,512,32]{1,2,0:T(8,128)S(1)}, f32[2,512,32]{1,2,0:T(8,128)S(1)}, u32[]{:S(2)}, u32[]{:S(2)}) collective-permute-start(f32[2,512,32]{1,2,0:T(8,128)S(1)} %fusion.59), channel_id=1, source_target_pairs={{2,0},{4,2},{6,4},{8,6},{10,8},{12,10},{14,12},{16,14},{18,16},{20... | collective-permute-start | bytes 393224 | tf_op jit(solution)/shard_map/ppermute | solution.py:19
  110.7 17.5 %collective-permute-start.2 = (f32[2,512,32]{1,2,0:T(8,128)S(1)}, f32[2,512,32]{1,2,0:T(8,128)S(1)}, u32[]{:S(2)}, u32[]{:S(2)}) collective-permute-start(f32[2,512,32]{1,2,0:T(8,128)S(1)} %fusion.59), channel_id=1, source_target_pairs={{0,2},{2,4},{4,6},{6,8},{8,10},{10,12},{12,14},{14,16},{16,18},{18... | collective-permute-start | bytes 393224 | tf_op jit(solution)/shard_map/ppermute | solution.py:18
Sparse Core Ops, SparseCore 0:
  12.9 10.8 all-gather.1
  102.2 24.5 all-reduce.1
where the time goes:
time: 159 us; the launch traced here: 157 us
  waiting for transfers between devices  61 us (38%)
  matrix products  38 us (24%)
  starting transfers between devices  16.5 us (10%)
  between operations  14.3 us (9%)
  other arithmetic  12.6 us (8%)
  blocking collectives  12.2 us (8%)
  local copies, waits for them, and re-layouts  2.51 us (2%)
    dot_general x17, matrix products, exact_einsum(): jnp.einsum(form, left, right, precision=lax.Precision.HIGHEST, preferred_...  35.8 us
    ppermute x2, waiting for transfers between devices, extended(): after = lax.ppermute(initial, axis, down)  19.5 us
    ppermute x2, waiting for transfers between devices, extended(): before = lax.ppermute(last, axis, up)  16.5 us
    psum x1, waiting for transfers between devices, shards(): coupled_sum, driven_sum = lax.psum((coupled_part, driven_part), 'grp')  14.1 us
    ppermute x2, starting transfers between devices, extended(): after = lax.ppermute(initial, axis, down)  12.6 us
    all_gather x1, waiting for transfers between devices, shards(): own_whole = lax.all_gather(outgoing, 'grp', axis=1, tiled=True)  10.9 us
    another operation x4, other arithmetic, shards(): chol_lower = jnp.linalg.cholesky(gram_total)  6.03 us
    another operation x3, other arithmetic, shards(): lax.linalg.triangular_solve(chol_lower, sketched, left_side=False, lower=...  5 us
  transfers between devices with their start and end apart: 6, of which 4 were waited for; matrix products, arithmetic and copies ran while one was open for 6% of the time, Pallas kernels for 0%

commit v1 on v0

v1 whole, which is shorter than its diff:
```python
import functools
import math

import jax
import jax.numpy as jnp
from jax import lax
from jax.experimental import pallas as pl
from jax.experimental.pallas import tpu as pltpu
from jax.sharding import PartitionSpec as P

MESH = pl.DeviceIdType.MESH
F32, BF16 = jnp.float32, jnp.bfloat16

PIECES = (
    (0, 0, 1, 0),
    (0, 2, -1, 3),
    (0, 3, -1, 4),
    (0, 1, 0, 6),
    (1, 1, 1, 2),
    (1, 3, -1, 5),
    (1, 0, 1, 1),
    (1, 2, 0, 7),
)
USE = {0: (0, 0), 1: (1, 0), 2: (0, 1), 3: (1, 2), 4: (0, 3), 5: (1, 3), 6: (1, 1), 7: (0, 2)}


def nt(left, right):
    return lax.dot_general(left, right, (((1,), (1,)), ((), ())), preferred_element_type=F32)


def nn(left, right):
    return lax.dot_general(left, right, (((1,), (0,)), ((), ())), preferred_element_type=F32)


def terms(x, count):
    out = []
    for step in range(count):
        part = x.astype(BF16)
        out.append(part)
        if step < count - 1:
            x = x - part.astype(F32)
    return out


def stacked(x, count):
    return jnp.concatenate(terms(x, count), axis=0)


def folded(x, count):
    size = x.shape[0] // count
    total = x[:size]
    for step in range(1, count):
        total = total + x[step * size : (step + 1) * size]
    return total


def exact_nt(left, right, count):
    rows = left.shape[0]
    ls, rs = terms(left, count), terms(right, count)
    total = None
    for order in range(count):
        got = nt(jnp.concatenate(ls[: count - order], axis=0), rs[order])
        got = folded(got, count - order)
        total = got if total is None else total + got
    return total


def exact_nn(left, right, count):
    ls, rs = terms(left, count), terms(right, count)
    total = None
    for order in range(count):
        got = nn(jnp.concatenate(ls[: count - order], axis=0), rs[order])
        got = folded(got, count - order)
        total = got if total is None else total + got
    return total


def inverse_factors(grams):
    size = grams[0].shape[0]
    row = lax.broadcasted_iota(jnp.int32, (size, size), 0)
    col = lax.broadcasted_iota(jnp.int32, (size, size), 1)
    eye = (row == col).astype(F32)
    down = lax.broadcasted_iota(jnp.int32, (size, 1), 0)
    work = [jnp.concatenate([gram, eye], axis=1) for gram in grams]
    for k in range(size - 1):
        for n, a in enumerate(work):
            line = a[k : k + 1, :] / a[k : k + 1, k : k + 1]
            lead = jnp.where(down > k, a[:, k : k + 1], 0.0)
            work[n] = a - lead * line
    out = []
    for a in work:
        diag = jnp.sum(jnp.where(row == col, a[:, :size], 0.0), axis=1, keepdims=True)
        out.append(a[:, size:] / jnp.sqrt(diag))
    return out


def kernel(
    g_size, b_size, ex, inv, coup, mask, sketch, bases_o, rc_o, re_o,
    ex_v, inv_v, c_v, sk_v, out_v, buf, src, skt, near, lin, lin_near, wbuf, y_v, bases_v, rc_v, re_v,
    load_sem, store_sem, p1_send, p1_recv, p1_fsend, p1_frecv, src_send, src_recv,
    sk_send, sk_recv, skp_send, skp_recv, skf_send, skf_recv, lin_send, lin_recv, w_send, w_recv,
):
    b, g = lax.axis_index("blk"), lax.axis_index("grp")
    has_left, has_right = b > 0, b < b_size - 1
    blocks, unknowns, _ = ex.shape
    rows = inv.shape[1]
    slots = coup.shape[1]
    r = sketch.shape[2]
    peers = [lax.rem(g + d, g_size) for d in range(1, g_size)]

    def load(number, source, target):
        return pltpu.make_async_copy(source, target, load_sem.at[number])

    loads = {}
    loads["sketch"] = load(0, sketch, sk_v)
    for i in range(blocks):
        loads["inv", i] = load(1 + 2 * i, inv.at[i], inv_v.at[i])
        loads["ex", i] = load(2 + 2 * i, ex.at[i], ex_v.at[i])
    for number, place in enumerate((6, 7, 0, 3, 4, 2, 5, 1)):
        i, k = USE[place]
        loads["c", i, k] = load(1 + 2 * blocks + number, coup.at[i, k], c_v.at[i, k])
    for copy in loads.values():
        copy.start()

    barrier = pltpu.get_barrier_semaphore()

    @pl.when(has_left)
    def _():
        pl.semaphore_signal(barrier, inc=1, device_id=(b - 1, g), device_id_type=MESH)

    @pl.when(has_right)
    def _():
        pl.semaphore_signal(barrier, inc=1, device_id=(b + 1, g), device_id_type=MESH)

    for peer in peers:
        pl.semaphore_signal(barrier, inc=1, device_id=(b, peer), device_id_type=MESH)
    pl.semaphore_wait(barrier, g_size - 1 + has_left.astype(jnp.int32) + has_right.astype(jnp.int32))

    def remote(source, target, send, recv, device):
        return pltpu.make_async_remote_copy(
            src_ref=source, dst_ref=target, send_sem=send, recv_sem=recv,
            device_id=device, device_id_type=MESH,
        )

    def to_peers(source, target, send, recv):
        return [
            remote(source, target, send.at[d], recv.at[d], (b, peer)) for d, peer in enumerate(peers)
        ]

    def there(direction):
        return has_left if direction > 0 else has_right

    def sends(direction):
        return has_right if direction > 0 else has_left

    @pl.when(jnp.logical_not(has_left))
    def _():
        for p in range(g_size):
            buf[p, 0 : 3 * r, :] = jnp.zeros((3 * r, rows), F32)
            near[0, p] = jnp.zeros((2 * r, rows), F32)
        lin_near[0] = jnp.zeros(lin_near.shape[1:], F32)

    @pl.when(jnp.logical_not(has_right))
    def _():
        for p in range(g_size):
            buf[p, 3 * r : 6 * r, :] = jnp.zeros((3 * r, rows), F32)
            near[1, p] = jnp.zeros((2 * r, rows), F32)
        lin_near[1] = jnp.zeros(lin_near.shape[1:], F32)

    loads["sketch"].wait()
    order = list(range(1, slots + 1)) + [0]
    flat = jnp.concatenate([sk_v[k].T for k in order], axis=0)
    flat_hi, flat_lo = terms(flat, 2)
    flat_both = jnp.concatenate([flat_hi, flat_lo], axis=0)

    piece_copies, own_copies = {}, {}
    for i in range(blocks):
        loads["inv", i].wait()
        loads["ex", i].wait()
        primary = nn(inv_v[i], ex_v[i])
        primary_hi, primary_lo = terms(primary, 2)
        got = folded(nt(flat_both, primary_hi), 2) + nt(flat_hi, primary_lo)
        out_v[i] = got
        for number, (block, slot, direction, place) in enumerate(PIECES):
            if block != i:
                continue
            here = buf.at[g, pl.ds(place * r, r)]
            if direction == 0:
                buf[g, pl.ds(place * r, r), :] = got[slot * r : (slot + 1) * r]
                own_copies[place] = to_peers(here, here, p1_fsend.at[place], p1_frecv.at[place])
                for copy in own_copies[place]:
                    copy.start()
            else:
                copy = remote(
                    out_v.at[i, pl.ds(slot * r, r)], here, p1_send.at[place], p1_recv.at[place],
                    (b + direction, g),
                )
                piece_copies[place] = (direction, copy)
                pl.when(sends(direction))(copy.start)

    def coupled(i, k, parts):
        total = None
        for p in range(g_size):
            got = nt(stacked(parts[p], 3), c_v[i, k, :, p * rows : (p + 1) * rows])
            total = got if total is None else total + got
        return folded(total, 3)

    weights = [[mask[i, k].astype(F32) for k in range(slots)] for i in range(blocks)]
    sources = [None] * blocks

    def add_source(place):
        i, k = USE[place]
        loads["c", i, k].wait()
        term = weights[i][k] * coupled(i, k, [buf[p, place * r : (place + 1) * r, :] for p in range(g_size)])
        sources[i] = term if sources[i] is None else sources[i] + term

    def forward(places):
        for place in places:
            direction, copy = piece_copies[place]
            here = buf.at[g, pl.ds(place * r, r)]
            own_copies[place] = to_peers(here, here, p1_fsend.at[place], p1_frecv.at[place])

            @pl.when(there(direction))
            def _():
                copy.wait_recv()
                for out in own_copies[place]:
                    out.start()

    def arrived(place):
        if place in piece_copies:

            @pl.when(there(piece_copies[place][0]))
            def _():
                for out in own_copies[place]:
                    out.wait_recv()
        else:
            for out in own_copies[place]:
                out.wait_recv()

    src_copies, sk_copies, skp_copies = {}, {}, {}

    def finish_source(i):
        src[g, i * r : (i + 1) * r, :] = sources[i]
        here = src.at[g, pl.ds(i * r, r)]
        src_copies[i] = to_peers(here, here, src_send.at[i], src_recv.at[i])
        for copy in src_copies[i]:
            copy.start()

    for place in (6, 7):
        arrived(place)
        add_source(place)
    forward((0, 3, 4))
    arrived(0)
    add_source(0)
    forward((2, 5))
    arrived(3)
    add_source(3)
    arrived(4)
    add_source(4)
    forward((1,))
    arrived(2)
    add_source(2)
    finish_source(0)
    arrived(5)
    add_source(5)
    arrived(1)
    add_source(1)
    finish_source(1)

    for i in range(blocks):
        for copy in src_copies[i]:
            copy.wait_recv()
        total = None
        for p in range(g_size):
            got = nt(
                stacked(src[p, i * r : (i + 1) * r, :], 3), inv_v[i, :, p * rows : (p + 1) * rows]
            )
            total = got if total is None else total + got
        skt[g, i * r : (i + 1) * r, :] = out_v[i, slots * r : (slots + 1) * r, :] - folded(total, 3)
        here = skt.at[g, pl.ds(i * r, r)]
        for side, direction in enumerate((1, -1)):
            copy = remote(
                here, near.at[side, g, pl.ds(i * r, r)], sk_send.at[side, i], sk_recv.at[side, i],
                (b + direction, g),
            )
            sk_copies[side, i] = (direction, copy)
            pl.when(sends(direction))(copy.start)
        skp_copies[i] = to_peers(here, here, skp_send.at[i], skp_recv.at[i])
        for copy in skp_copies[i]:
            copy.start()

    grams = []
    for i in range(blocks):
        for copy in skp_copies[i]:
            copy.wait_recv()
        total = None
        for p in range(g_size):
            part = skt[p, i * r : (i + 1) * r, :]
            got = exact_nt(part, part, 3)
            total = got if total is None else total + got
        grams.append(total * (1.0 / unknowns))
    inverses = inverse_factors(grams)
    for i in range(blocks):
        lin[i * r : (i + 1) * r, :] = jnp.concatenate([inverses[i]] * slots, axis=1)
    lin_copies = []
    for side, direction in enumerate((1, -1)):
        copy = remote(lin, lin_near.at[side], lin_send.at[side], lin_recv.at[side], (b + direction, g))
        lin_copies.append((direction, copy))
        pl.when(sends(direction))(copy.start)

    skf_copies = {}

    def forward_sketched(side, i):
        direction, copy = sk_copies[side, i]
        here = near.at[side, g, pl.ds(i * r, r)]
        skf_copies[side, i] = to_peers(here, here, skf_send.at[side, i], skf_recv.at[side, i])

        @pl.when(there(direction))
        def _():
            copy.wait_recv()
            for out in skf_copies[side, i]:
                out.start()

    def arrived_sketched(side, i):
        @pl.when(there(sk_copies[side, i][0]))
        def _():
            for out in skf_copies[side, i]:
                out.wait_recv()

    for side in range(2):
        forward_sketched(side, 0)

    scale = 1.0 / math.sqrt(unknowns)
    bases_t = []
    for i in range(blocks):
        own = exact_nn(inverses[i], skt[g, i * r : (i + 1) * r, :], 3)
        bases_t.append(own)
        bases_v[i] = own.T
        driven = None
        for p in range(g_size):
            got = nn(stacked(skt[p, i * r : (i + 1) * r, :], 3), ex_v[i, p * rows : (p + 1) * rows, :])
            driven = got if driven is None else driven + got
        re_v[i] = exact_nn(inverses[i], folded(driven, 3), 3) * scale
    stores = [
        pltpu.make_async_copy(bases_v, bases_o, store_sem.at[0]),
        pltpu.make_async_copy(re_v, re_o, store_sem.at[1]),
    ]
    for copy in stores:
        copy.start()

    def couple_basis(i, k, parts):
        y_v[i, k * r : (k + 1) * r, :] = coupled(i, k, parts)

    couple_basis(0, 2, [skt[p, r : 2 * r, :] for p in range(g_size)])
    for side in range(2):
        forward_sketched(side, 1)
    couple_basis(1, 1, [skt[p, 0:r, :] for p in range(g_size)])

    arrived_sketched(0, 0)
    couple_basis(0, 0, [near[0, p, 0:r, :] for p in range(g_size)])
    arrived_sketched(1, 0)
    parts = [near[1, p, 0:r, :] for p in range(g_size)]
    couple_basis(0, 3, parts)
    couple_basis(1, 2, parts)
    arrived_sketched(0, 1)
    parts = [near[0, p, r : 2 * r, :] for p in range(g_size)]
    couple_basis(0, 1, parts)
    couple_basis(1, 0, parts)
    arrived_sketched(1, 1)
    couple_basis(1, 3, [near[1, p, r : 2 * r, :] for p in range(g_size)])

    for direction, copy in lin_copies:
        pl.when(there(direction))(copy.wait_recv)

    wide = slots * r
    row = lax.broadcasted_iota(jnp.int32, (wide, wide), 0) // r
    col = lax.broadcasted_iota(jnp.int32, (wide, wide), 1) // r
    left_a, left_b = lin_near[0, 0:r, :], lin_near[0, r : 2 * r, :]
    right_a, right_b = lin_near[1, 0:r, :], lin_near[1, r : 2 * r, :]
    own_a, own_b = lin[0:r, :], lin[r : 2 * r, :]
    beside = ((left_a, left_b, own_b, right_a), (left_b, own_a, right_a, right_b))
    for i in range(blocks):
        product = exact_nt(bases_t[i], y_v[i], 3)
        factors = jnp.where(row == col, jnp.concatenate(beside[i], axis=0), 0.0)
        wbuf[g, i * r : (i + 1) * r, :] = exact_nt(product, factors, 3)
    here = wbuf.at[g]
    w_copies = to_peers(here, here, w_send, w_recv)
    for copy in w_copies:
        copy.start()
    for copy in w_copies:
        copy.wait_recv()
    total = wbuf[0]
    for p in range(1, g_size):
        total = total + wbuf[p]
    total = total * scale
    for i in range(blocks):
        for k in range(slots):
            rc_v[i, k] = total[i * r : (i + 1) * r, k * r : (k + 1) * r]
    last = pltpu.make_async_copy(rc_v, rc_o, store_sem.at[2])
    last.start()

    for direction, copy in list(piece_copies.values()) + list(sk_copies.values()) + lin_copies:
        pl.when(sends(direction))(copy.wait_send)
    for place, copies in own_copies.items():
        for copy in copies:
            if place in piece_copies:
                pl.when(there(piece_copies[place][0]))(copy.wait_send)
            else:
                copy.wait_send()
    for (side, i), copies in skf_copies.items():
        for copy in copies:
            pl.when(there(sk_copies[side, i][0]))(copy.wait_send)
    for copies in list(src_copies.values()) + list(skp_copies.values()) + [w_copies]:
        for copy in copies:
            copy.wait_send()
    for copy in stores:
        copy.wait()
    last.wait()


def shards(g_size, b_size, excitation, inverse_self, coupling, neighbour_mask, sketch):
    blocks, unknowns, columns = excitation.shape
    rows = inverse_self.shape[1]
    slots = coupling.shape[1]
    r = sketch.shape[2]
    assert blocks == 2 and slots == 4 and rows * g_size == unknowns
    others = max(g_size - 1, 1)
    wide = slots * r
    vmem = lambda *shape: pltpu.VMEM(shape, F32)
    dma = lambda *shape: pltpu.SemaphoreType.DMA(shape)
    anywhere = pl.BlockSpec(memory_space=pl.ANY)
    flops = 2 * blocks * rows * unknowns * (columns + 2 * slots * 3 * r)
    return pl.pallas_call(
        functools.partial(kernel, g_size, b_size),
        out_shape=(
            jax.ShapeDtypeStruct((blocks, rows, r), F32),
            jax.ShapeDtypeStruct((blocks, slots, r, r), F32),
            jax.ShapeDtypeStruct((blocks, r, columns), F32),
        ),
        in_specs=[anywhere, anywhere, anywhere, pl.BlockSpec(memory_space=pltpu.SMEM), anywhere],
        out_specs=(anywhere, anywhere, anywhere),
        scratch_shapes=[
            pltpu.VMEM(excitation.shape, BF16),
            pltpu.VMEM(inverse_self.shape, BF16),
            pltpu.VMEM(coupling.shape, BF16),
            vmem(*sketch.shape),
            vmem(blocks, (slots + 1) * r, rows),
            vmem(g_size, 8 * r, rows),
            vmem(g_size, 2 * r, rows),
            vmem(g_size, 2 * r, rows),
            vmem(2, g_size, 2 * r, rows),
            vmem(2 * r, wide),
            vmem(2, 2 * r, wide),
            vmem(g_size, 2 * r, wide),
            vmem(blocks, wide, rows),
            vmem(blocks, rows, r),
            vmem(blocks, slots, r, r),
            vmem(blocks, r, columns),
            dma(1 + 2 * blocks + blocks * slots),
            dma(3),
            dma(6),
            dma(6),
            dma(8, others),
            dma(8, others),
            dma(blocks, others),
            dma(blocks, others),
            dma(2, blocks),
            dma(2, blocks),
            dma(blocks, others),
            dma(blocks, others),
            dma(2, blocks, others),
            dma(2, blocks, others),
            dma(2),
            dma(2),
            dma(others),
            dma(others),
        ],
        compiler_params=pltpu.CompilerParams(
            collective_id=0, has_side_effects=True, vmem_limit_bytes=48 * 1024 * 1024
        ),
        cost_estimate=pl.CostEstimate(
            flops=flops, bytes_accessed=2 * (coupling.size + inverse_self.size), transcendentals=0
        ),
        name="basis_currents",
    )(excitation, inverse_self, coupling, neighbour_mask, sketch)


def solution(mesh):
    return jax.shard_map(
        functools.partial(shards, mesh.shape["grp"], mesh.shape["blk"]),
        mesh=mesh,
        in_specs=(
            P("blk", None, None),
            P("blk", "grp", None),
            P("blk", None, "grp", None),
            P("blk", None),
            P(),
        ),
        out_specs=(P("blk", "grp", None), P("blk", None, None, None), P("blk", None, None)),
        check_vma=False,
    )
```

time: 159 us -> 39.4 us (0.25)
  waiting for transfers between devices: 61 us -> 0 us
  matrix products: 38 us -> 0 us
  Pallas kernels: 0 us -> 31.2 us
  starting transfers between devices: 16.5 us -> 0 us
  between operations: 14.3 us -> 0.66 us
  other arithmetic: 12.6 us -> 0 us
  blocking collectives: 12.2 us -> 0 us
  local copies, waits for them, and re-layouts: 2.51 us -> 6.75 us
    dot_general x18 -> x0, matrix products: 37.7 us -> none  [the longest x17 35.8 us: exact_einsum(): jnp.einsum(form, left, right, precision=lax.Precision.HIGHEST, preferred_...]
    ppermute x4 -> x0, waiting for transfers between devices: 36 us -> none  [the longest x2 19.5 us: extended(): after = lax.ppermute(initial, axis, down)]
    pallas_call x0 -> x1, Pallas kernels: none -> 31.2 us  [shards(): pl.pallas_call(functools.partial(kernel, g_size, b_size), out_shape=(jax....]
    ppermute x4 -> x0, starting transfers between devices: 16.5 us -> none  [the longest x2 12.6 us: extended(): after = lax.ppermute(initial, axis, down)]
    psum x1 -> x0, waiting for transfers between devices: 14.1 us -> none  [shards(): coupled_sum, driven_sum = lax.psum((coupled_part, driven_part), 'grp')]
    another operation x8 -> x0, other arithmetic: 11 us -> none  [the longest x4 6.03 us: shards(): chol_lower = jnp.linalg.cholesky(gram_total)]
    all_gather x1 -> x0, waiting for transfers between devices: 10.9 us -> none  [shards(): own_whole = lax.all_gather(outgoing, 'grp', axis=1, tiled=True)]
    psum x2 -> x0, blocking collectives: 7.4 us -> none  [the longest x1 3.8 us: shards(): coupled_sum, driven_sum = lax.psum((coupled_part, driven_part), 'grp')]
  transfers between devices with their start and end apart: 6 -> 0, of which waited for: 4 -> 0; matrix products, arithmetic and copies ran while one was open for 6% -> 0% of each run, Pallas kernels for 0% -> 0%
where the time goes in v1:
time: 39.4 us; the launch traced here: 38.7 us
  Pallas kernels  31.2 us (79%)
  local copies, waits for them, and re-layouts  6.75 us (17%)
  between operations  0.66 us (2%)
    pallas_call x1, Pallas kernels, shards(): pl.pallas_call(functools.partial(kernel, g_size, b_size), out_shape=(jax....  31.2 us
    unnamed x9, local copies, waits for them, and re-layouts  5.92 us
    pallas_call x1, local copies, waits for them, and re-layouts, shards(): pl.pallas_call(functools.partial(kernel, g_size, b_size), out_shape=(jax....  0.83 us

profile of v1, /device:TPU:17, one launch (start us, length us, event | category | flops | bytes accessed | tf_op | source)
XLA Modules:
  0.0 38.7 jit_solution(10286184482068537913)
XLA Ops:
  0.6 1.1 %copy.8.sketch = f32[5,256,32]{2,1,0:T(8,128)S(1)} copy(f32[5,256,32]{1,2,0:T(8,128)} %param.9) | data formatting | bytes 327680 | tf_op args[4]
  1.8 0.0 copy-start
  1.8 1.6 %copy-done = bf16[2,512,1024]{2,1,0:T(8,128)(2,1)S(1)} copy-done((bf16[2,512,1024]{2,1,0:T(8,128)(2,1)S(1)}, bf16[2,512,1024]{2,1,0:T(8,128)(2,1)}, u32[]{:S(2)}) %copy-start) | copy-done | bytes 2097176
  3.4 0.0 copy-start.1
  3.4 1.2 %copy-done.1 = bf16[2,1024,256]{2,1,0:T(8,128)(2,1)S(1)} copy-done((bf16[2,1024,256]{2,1,0:T(8,128)(2,1)S(1)}, bf16[2,1024,256]{2,1,0:T(8,128)(2,1)}, u32[]{:S(2)}) %copy-start.1) | copy-done | bytes 1048600
  4.6 0.0 copy-start.2
  4.6 0.7 %copy-done.2 = s32[2,4]{1,0:T(2,128)S(1)} copy-done((s32[2,4]{1,0:T(2,128)S(1)}, s32[2,4]{1,0:T(2,128)}, u32[]{:S(2)}) %copy-start.2) | copy-done | bytes 56
  5.3 31.2 %basis_currents.1 = (f32[2,512,32]{2,1,0:T(8,128)S(1)}, f32[2,4,32,32]{3,2,1,0:T(8,128)S(1)}, f32[2,32,256]{2,1,0:T(8,128)S(1)}) custom-call(bf16[2,1024,256]{2,1,0:T(8,128)(2,1)S(1)} %copy-done.1, bf16[2,512,1024]{2,1,0:T(8,128)(2,1)S(1)} %copy-done, bf16[2,4,512,1024]{3,2,1,0:T(8,128)(2,1)} %coup.1, s32[2,4]{1,0:T(2,128)S(1)} %copy-done.2, ...), custom_call_target="tpu_custom_call" | custom-call | flops 2147483648 | bytes 10485760 | tf_op jit(solution)/shard_map/basis_currents/pallas_call | solution.py:433
  36.5 0.8 %copy.9 = f32[2,512,32]{1,2,0:T(8,128)} copy(f32[2,512,32]{2,1,0:T(8,128)S(1)} %get-tuple-element.3) | data formatting | bytes 262144 | tf_op jit(solution)/shard_map/basis_currents/pallas_call | solution.py:433
  37.4 0.7 %copy.12 = f32[2,4,32,32]{3,2,1,0:T(8,128)} copy(f32[2,4,32,32]{3,2,1,0:T(8,128)S(1)} %get-tuple-element.10) | data formatting | bytes 65536
  38.0 0.6 %copy.13 = f32[2,32,256]{2,1,0:T(8,128)} copy(f32[2,32,256]{2,1,0:T(8,128)S(1)} %get-tuple-element.11) | data formatting | bytes 131072
Async XLA Ops:
  1.8 1.6 %copy-start = (bf16[2,512,1024]{2,1,0:T(8,128)(2,1)S(1)}, bf16[2,512,1024]{2,1,0:T(8,128)(2,1)}, u32[]{:S(2)}) copy-start(bf16[2,512,1024]{2,1,0:T(8,128)(2,1)} %inv.1) | copy-start | bytes 6291460
  3.4 1.2 %copy-start.1 = (bf16[2,1024,256]{2,1,0:T(8,128)(2,1)S(1)}, bf16[2,1024,256]{2,1,0:T(8,128)(2,1)}, u32[]{:S(2)}) copy-start(bf16[2,1024,256]{2,1,0:T(8,128)(2,1)} %ex.1) | copy-start | bytes 3145732
  4.6 0.7 %copy-start.2 = (s32[2,4]{1,0:T(2,128)S(1)}, s32[2,4]{1,0:T(2,128)}, u32[]{:S(2)}) copy-start(s32[2,4]{1,0:T(2,128)} %mask.1) | copy-start | bytes 100

commit v2 on v1

--- a/solution.py
+++ b/solution.py
@@ -13,13 +13,13 @@
 
 PIECES = (
     (0, 0, 1, 0),
-    (0, 2, -1, 3),
     (0, 3, -1, 4),
     (0, 1, 0, 6),
     (1, 1, 1, 2),
+    (1, 2, 0, 7),
+    (0, 2, -1, 3),
+    (1, 0, 1, 1),
     (1, 3, -1, 5),
-    (1, 0, 1, 1),
-    (1, 2, 0, 7),
 )
 USE = {0: (0, 0), 1: (1, 0), 2: (0, 1), 3: (1, 2), 4: (0, 3), 5: (1, 3), 6: (1, 1), 7: (0, 2)}
 
@@ -96,16 +96,16 @@
 
 def kernel(
     g_size, b_size, ex, inv, coup, mask, sketch, bases_o, rc_o, re_o,
-    ex_v, inv_v, c_v, sk_v, out_v, buf, src, skt, near, lin, lin_near, wbuf, y_v, bases_v, rc_v, re_v,
+    ex_v, inv_v, c_v, sk_v, out_v, buf, src, skt, near, lin, lin_near, wbuf, v_out, v_in, bases_v, rc_v, re_v,
     load_sem, store_sem, p1_send, p1_recv, p1_fsend, p1_frecv, src_send, src_recv,
-    sk_send, sk_recv, skp_send, skp_recv, skf_send, skf_recv, lin_send, lin_recv, w_send, w_recv,
+    sk_send, sk_recv, skp_send, skp_recv, v_send, v_recv, lin_send, lin_recv, w_send, w_recv,
 ):
     b, g = lax.axis_index("blk"), lax.axis_index("grp")
     has_left, has_right = b > 0, b < b_size - 1
     blocks, unknowns, _ = ex.shape
     rows = inv.shape[1]
     slots = coup.shape[1]
-    r = sketch.shape[2]
+    r = sketch.shape[1]
     peers = [lax.rem(g + d, g_size) for d in range(1, g_size)]
 
     def load(number, source, target):
@@ -116,7 +116,7 @@
     for i in range(blocks):
         loads["inv", i] = load(1 + 2 * i, inv.at[i], inv_v.at[i])
         loads["ex", i] = load(2 + 2 * i, ex.at[i], ex_v.at[i])
-    for number, place in enumerate((6, 7, 0, 3, 4, 2, 5, 1)):
+    for number, place in enumerate((7, 6, 0, 4, 2, 3, 1, 5)):
         i, k = USE[place]
         loads["c", i, k] = load(1 + 2 * blocks + number, coup.at[i, k], c_v.at[i, k])
     for copy in loads.values():
@@ -134,7 +134,6 @@
 
     for peer in peers:
         pl.semaphore_signal(barrier, inc=1, device_id=(b, peer), device_id_type=MESH)
-    pl.semaphore_wait(barrier, g_size - 1 + has_left.astype(jnp.int32) + has_right.astype(jnp.int32))
 
     def remote(source, target, send, recv, device):
         return pltpu.make_async_remote_copy(
@@ -157,46 +156,50 @@
     def _():
         for p in range(g_size):
             buf[p, 0 : 3 * r, :] = jnp.zeros((3 * r, rows), F32)
-            near[0, p] = jnp.zeros((2 * r, rows), F32)
+        near[0] = jnp.zeros(near.shape[1:], F32)
         lin_near[0] = jnp.zeros(lin_near.shape[1:], F32)
 
     @pl.when(jnp.logical_not(has_right))
     def _():
         for p in range(g_size):
             buf[p, 3 * r : 6 * r, :] = jnp.zeros((3 * r, rows), F32)
-            near[1, p] = jnp.zeros((2 * r, rows), F32)
+        near[1] = jnp.zeros(near.shape[1:], F32)
         lin_near[1] = jnp.zeros(lin_near.shape[1:], F32)
 
     loads["sketch"].wait()
     order = list(range(1, slots + 1)) + [0]
-    flat = jnp.concatenate([sk_v[k].T for k in order], axis=0)
+    flat = jnp.concatenate([sk_v[k] for k in order], axis=0)
     flat_hi, flat_lo = terms(flat, 2)
     flat_both = jnp.concatenate([flat_hi, flat_lo], axis=0)
 
     piece_copies, own_copies = {}, {}
+
+    def send_piece(block, slot, direction, place):
+        here = buf.at[g, pl.ds(place * r, r)]
+        if direction == 0:
+            buf[g, pl.ds(place * r, r), :] = out_v[block, slot * r : (slot + 1) * r, :]
+            own_copies[place] = to_peers(here, here, p1_fsend.at[place], p1_frecv.at[place])
+            for copy in own_copies[place]:
+                copy.start()
+        else:
+            copy = remote(
+                out_v.at[block, pl.ds(slot * r, r)], here, p1_send.at[place], p1_recv.at[place],
+                (b + direction, g),
+            )
+            piece_copies[place] = (direction, copy)
+            pl.when(sends(direction))(copy.start)
+
     for i in range(blocks):
         loads["inv", i].wait()
         loads["ex", i].wait()
         primary = nn(inv_v[i], ex_v[i])
         primary_hi, primary_lo = terms(primary, 2)
-        got = folded(nt(flat_both, primary_hi), 2) + nt(flat_hi, primary_lo)
-        out_v[i] = got
-        for number, (block, slot, direction, place) in enumerate(PIECES):
-            if block != i:
-                continue
-            here = buf.at[g, pl.ds(place * r, r)]
-            if direction == 0:
-                buf[g, pl.ds(place * r, r), :] = got[slot * r : (slot + 1) * r]
-                own_copies[place] = to_peers(here, here, p1_fsend.at[place], p1_frecv.at[place])
-                for copy in own_copies[place]:
-                    copy.start()
-            else:
-                copy = remote(
-                    out_v.at[i, pl.ds(slot * r, r)], here, p1_send.at[place], p1_recv.at[place],
-                    (b + direction, g),
-                )
-                piece_copies[place] = (direction, copy)
-                pl.when(sends(direction))(copy.start)
+        out_v[i] = folded(nt(flat_both, primary_hi), 2) + nt(flat_hi, primary_lo)
+        if i == 0:
+            neighbours = has_left.astype(jnp.int32) + has_right.astype(jnp.int32)
+            pl.semaphore_wait(barrier, g_size - 1 + neighbours)
+        for piece in PIECES[:3] if i == 0 else PIECES[3:]:
+            send_piece(*piece)
 
     def coupled(i, k, parts):
         total = None
@@ -237,7 +240,7 @@
             for out in own_copies[place]:
                 out.wait_recv()
 
-    src_copies, sk_copies, skp_copies = {}, {}, {}
+    src_copies, sk_copies, skp_copies, v_copies = {}, {}, {}, {}
 
     def finish_source(i):
         src[g, i * r : (i + 1) * r, :] = sources[i]
@@ -246,28 +249,7 @@
         for copy in src_copies[i]:
             copy.start()
 
-    for place in (6, 7):
-        arrived(place)
-        add_source(place)
-    forward((0, 3, 4))
-    arrived(0)
-    add_source(0)
-    forward((2, 5))
-    arrived(3)
-    add_source(3)
-    arrived(4)
-    add_source(4)
-    forward((1,))
-    arrived(2)
-    add_source(2)
-    finish_source(0)
-    arrived(5)
-    add_source(5)
-    arrived(1)
-    add_source(1)
-    finish_source(1)
-
-    for i in range(blocks):
+    def sketch_block(i):
         for copy in src_copies[i]:
             copy.wait_recv()
         total = None
@@ -280,7 +262,7 @@
         here = skt.at[g, pl.ds(i * r, r)]
         for side, direction in enumerate((1, -1)):
             copy = remote(
-                here, near.at[side, g, pl.ds(i * r, r)], sk_send.at[side, i], sk_recv.at[side, i],
+                here, near.at[side, pl.ds(i * r, r)], sk_send.at[side, i], sk_recv.at[side, i],
                 (b + direction, g),
             )
             sk_copies[side, i] = (direction, copy)
@@ -289,16 +271,65 @@
         for copy in skp_copies[i]:
             copy.start()
 
-    grams = []
+    def project(i, k):
+        got = folded(nn(stacked(skt[g, i * r : (i + 1) * r, :], 3), c_v[i, k]), 3)
+        for p in range(g_size):
+            v_out[p, (i * slots + k) * r : (i * slots + k + 1) * r, :] = got[:, p * rows : (p + 1) * rows]
+
+    def send_projected(i):
+        span = pl.ds(i * slots * r, slots * r)
+        v_copies[i] = [
+            remote(
+                v_out.at[peer, span], v_in.at[d, span], v_send.at[i, d], v_recv.at[i, d], (b, peer)
+            )
+            for d, peer in enumerate(peers)
+        ]
+        for copy in v_copies[i]:
+            copy.start()
+
+    for place in (7, 6):
+        arrived(place)
+        add_source(place)
+    forward((0, 4))
+    arrived(0)
+    add_source(0)
+    forward((2,))
+    arrived(4)
+    add_source(4)
+    arrived(2)
+    add_source(2)
+    finish_source(0)
+    forward((3,))
+    sketch_block(0)
+    forward((1, 5))
+    arrived(3)
+    add_source(3)
+    arrived(1)
+    add_source(1)
+    arrived(5)
+    add_source(5)
+    finish_source(1)
+    for k in range(slots):
+        project(0, k)
+    send_projected(0)
+    sketch_block(1)
+    for k in range(2):
+        project(1, k)
+
     for i in range(blocks):
         for copy in skp_copies[i]:
             copy.wait_recv()
+    grams = []
+    for i in range(blocks):
         total = None
         for p in range(g_size):
             part = skt[p, i * r : (i + 1) * r, :]
             got = exact_nt(part, part, 3)
             total = got if total is None else total + got
         grams.append(total * (1.0 / unknowns))
+    for k in range(2, slots):
+        project(1, k)
+    send_projected(1)
     inverses = inverse_factors(grams)
     for i in range(blocks):
         lin[i * r : (i + 1) * r, :] = jnp.concatenate([inverses[i]] * slots, axis=1)
@@ -308,34 +339,9 @@
         lin_copies.append((direction, copy))
         pl.when(sends(direction))(copy.start)
 
-    skf_copies = {}
-
-    def forward_sketched(side, i):
-        direction, copy = sk_copies[side, i]
-        here = near.at[side, g, pl.ds(i * r, r)]
-        skf_copies[side, i] = to_peers(here, here, skf_send.at[side, i], skf_recv.at[side, i])
-
-        @pl.when(there(direction))
-        def _():
-            copy.wait_recv()
-            for out in skf_copies[side, i]:
-                out.start()
-
-    def arrived_sketched(side, i):
-        @pl.when(there(sk_copies[side, i][0]))
-        def _():
-            for out in skf_copies[side, i]:
-                out.wait_recv()
-
-    for side in range(2):
-        forward_sketched(side, 0)
-
     scale = 1.0 / math.sqrt(unknowns)
-    bases_t = []
-    for i in range(blocks):
-        own = exact_nn(inverses[i], skt[g, i * r : (i + 1) * r, :], 3)
-        bases_t.append(own)
-        bases_v[i] = own.T
+    for i in range(blocks):
+        bases_v[i] = exact_nn(inverses[i], skt[g, i * r : (i + 1) * r, :], 3)
         driven = None
         for p in range(g_size):
             got = nn(stacked(skt[p, i * r : (i + 1) * r, :], 3), ex_v[i, p * rows : (p + 1) * rows, :])
@@ -348,40 +354,50 @@
     for copy in stores:
         copy.start()
 
-    def couple_basis(i, k, parts):
-        y_v[i, k * r : (k + 1) * r, :] = coupled(i, k, parts)
-
-    couple_basis(0, 2, [skt[p, r : 2 * r, :] for p in range(g_size)])
-    for side in range(2):
-        forward_sketched(side, 1)
-    couple_basis(1, 1, [skt[p, 0:r, :] for p in range(g_size)])
-
-    arrived_sketched(0, 0)
-    couple_basis(0, 0, [near[0, p, 0:r, :] for p in range(g_size)])
-    arrived_sketched(1, 0)
-    parts = [near[1, p, 0:r, :] for p in range(g_size)]
-    couple_basis(0, 3, parts)
-    couple_basis(1, 2, parts)
-    arrived_sketched(0, 1)
-    parts = [near[0, p, r : 2 * r, :] for p in range(g_size)]
-    couple_basis(0, 1, parts)
-    couple_basis(1, 0, parts)
-    arrived_sketched(1, 1)
-    couple_basis(1, 3, [near[1, p, r : 2 * r, :] for p in range(g_size)])
-
-    for direction, copy in lin_copies:
-        pl.when(there(direction))(copy.wait_recv)
-
     wide = slots * r
     row = lax.broadcasted_iota(jnp.int32, (wide, wide), 0) // r
     col = lax.broadcasted_iota(jnp.int32, (wide, wide), 1) // r
+    diagonal = row == col
+    projected = []
+    for i in range(blocks):
+        for copy in v_copies[i]:
+            copy.wait_recv()
+        span = slice(i * wide, (i + 1) * wide)
+        total = v_out[g, pl.ds(i * wide, wide), :]
+        for d in range(g_size - 1):
+            total = total + v_in[d, span, :]
+        factors = jnp.where(diagonal, jnp.concatenate([lin[i * r : (i + 1) * r, :]] * slots, axis=0), 0.0)
+        projected.append(exact_nn(factors, total, 3))
+
+    products = {}
+
+    def reduce(users, basis):
+        left = [projected[i][k * r : (k + 1) * r] for i, k in users]
+        got = exact_nt(left[0] if len(left) == 1 else jnp.concatenate(left, axis=0), basis, 3)
+        for n, user in enumerate(users):
+            products[user] = got[n * r : (n + 1) * r]
+
+    reduce([(1, 1)], skt[g, 0:r, :])
+    reduce([(0, 2)], skt[g, r : 2 * r, :])
+    for i, side, users in (
+        (0, 0, [(0, 0)]),
+        (0, 1, [(0, 3), (1, 2)]),
+        (1, 0, [(0, 1), (1, 0)]),
+        (1, 1, [(1, 3)]),
+    ):
+        direction, copy = sk_copies[side, i]
+        pl.when(there(direction))(copy.wait_recv)
+        reduce(users, near[side, i * r : (i + 1) * r, :])
+    for direction, copy in lin_copies:
+        pl.when(there(direction))(copy.wait_recv)
+
     left_a, left_b = lin_near[0, 0:r, :], lin_near[0, r : 2 * r, :]
     right_a, right_b = lin_near[1, 0:r, :], lin_near[1, r : 2 * r, :]
     own_a, own_b = lin[0:r, :], lin[r : 2 * r, :]
     beside = ((left_a, left_b, own_b, right_a), (left_b, own_a, right_a, right_b))
     for i in range(blocks):
-        product = exact_nt(bases_t[i], y_v[i], 3)
-        factors = jnp.where(row == col, jnp.concatenate(beside[i], axis=0), 0.0)
+        product = jnp.concatenate([products[i, k] for k in range(slots)], axis=1)
+        factors = jnp.where(diagonal, jnp.concatenate(beside[i], axis=0), 0.0)
         wbuf[g, i * r : (i + 1) * r, :] = exact_nt(product, factors, 3)
     here = wbuf.at[g]
     w_copies = to_peers(here, here, w_send, w_recv)
@@ -407,10 +423,7 @@
                 pl.when(there(piece_copies[place][0]))(copy.wait_send)
             else:
                 copy.wait_send()
-    for (side, i), copies in skf_copies.items():
-        for copy in copies:
-            pl.when(there(sk_copies[side, i][0]))(copy.wait_send)
-    for copies in list(src_copies.values()) + list(skp_copies.values()) + [w_copies]:
+    for copies in list(src_copies.values()) + list(skp_copies.values()) + list(v_copies.values()) + [w_copies]:
         for copy in copies:
             copy.wait_send()
     for copy in stores:
@@ -418,11 +431,23 @@
     last.wait()
 
 
+def hand_over(a, b, c, a_out, b_out, c_out, sems):
+    copies = [
+        pltpu.make_async_copy(source, target, sems.at[n])
+        for n, (source, target) in enumerate(((a, a_out), (b, b_out), (c, c_out)))
+    ]
+    for copy in copies:
+        copy.start()
+    for copy in copies:
+        copy.wait()
+
+
 def shards(g_size, b_size, excitation, inverse_self, coupling, neighbour_mask, sketch):
     blocks, unknowns, columns = excitation.shape
     rows = inverse_self.shape[1]
     slots = coupling.shape[1]
-    r = sketch.shape[2]
+    sketch = jnp.swapaxes(sketch, 1, 2)
+    r = sketch.shape[1]
     assert blocks == 2 and slots == 4 and rows * g_size == unknowns
     others = max(g_size - 1, 1)
     wide = slots * r
@@ -430,10 +455,10 @@
     dma = lambda *shape: pltpu.SemaphoreType.DMA(shape)
     anywhere = pl.BlockSpec(memory_space=pl.ANY)
     flops = 2 * blocks * rows * unknowns * (columns + 2 * slots * 3 * r)
-    return pl.pallas_call(
+    bases, reduced, driven = pl.pallas_call(
         functools.partial(kernel, g_size, b_size),
         out_shape=(
-            jax.ShapeDtypeStruct((blocks, rows, r), F32),
+            jax.ShapeDtypeStruct((blocks, r, rows), F32),
             jax.ShapeDtypeStruct((blocks, slots, r, r), F32),
             jax.ShapeDtypeStruct((blocks, r, columns), F32),
         ),
@@ -448,12 +473,13 @@
             vmem(g_size, 8 * r, rows),
             vmem(g_size, 2 * r, rows),
             vmem(g_size, 2 * r, rows),
-            vmem(2, g_size, 2 * r, rows),
+            vmem(2, 2 * r, rows),
             vmem(2 * r, wide),
             vmem(2, 2 * r, wide),
             vmem(g_size, 2 * r, wide),
-            vmem(blocks, wide, rows),
-            vmem(blocks, rows, r),
+            vmem(g_size, blocks * wide, rows),
+            vmem(others, blocks * wide, rows),
+            vmem(blocks, r, rows),
             vmem(blocks, slots, r, r),
             vmem(blocks, r, columns),
             dma(1 + 2 * blocks + blocks * slots),
@@ -468,21 +494,32 @@
             dma(2, blocks),
             dma(blocks, others),
             dma(blocks, others),
-            dma(2, blocks, others),
-            dma(2, blocks, others),
+            dma(blocks, others),
+            dma(blocks, others),
             dma(2),
             dma(2),
             dma(others),
             dma(others),
         ],
         compiler_params=pltpu.CompilerParams(
-            collective_id=0, has_side_effects=True, vmem_limit_bytes=48 * 1024 * 1024
+            collective_id=0, has_side_effects=True, vmem_limit_bytes=60 * 1024 * 1024
         ),
         cost_estimate=pl.CostEstimate(
             flops=flops, bytes_accessed=2 * (coupling.size + inverse_self.size), transcendentals=0
         ),
         name="basis_currents",
     )(excitation, inverse_self, coupling, neighbour_mask, sketch)
+    results = (bases, reduced, driven)
+    bases, reduced, driven = pl.pallas_call(
+        hand_over,
+        out_shape=tuple(jax.ShapeDtypeStruct(x.shape, x.dtype) for x in results),
+        in_specs=[anywhere] * 3,
+        out_specs=(anywhere,) * 3,
+        scratch_shapes=[dma(3)],
+        compiler_params=pltpu.CompilerParams(vmem_limit_bytes=60 * 1024 * 1024),
+        name="hand_over",
+    )(*results)
+    return jnp.swapaxes(bases, 1, 2), reduced, driven
 
 
 def solution(mesh):

time: 39.4 us -> 41.5 us (1.053); the launches traced: 38.7 us -> 41.4 us
  Pallas kernels: 31.2 us -> 40.7 us
  local copies, waits for them, and re-layouts: 6.75 us -> 0 us
    pallas_call x0 -> x1, Pallas kernels: none -> 11.1 us  [shards(): pl.pallas_call(hand_over, out_shape=tuple((jax.ShapeDtypeStruct(x.shape,...]
    unnamed x9 -> x0, local copies, waits for them, and re-layouts: 5.92 us -> none
    pallas_call x1, Pallas kernels: 31.2 us -> 29.7 us  [shards(): pl.pallas_call(functools.partial(kernel, g_size, b_size), out_shape=(jax....]
    pallas_call x1 -> x0, local copies, waits for them, and re-layouts: 0.83 us -> none  [shards(): pl.pallas_call(functools.partial(kernel, g_size, b_size), out_shape=(jax....]
where the time goes in v2:
time: 41.5 us; the launch traced here: 41.4 us
  Pallas kernels  40.7 us (98%)
  between operations  0.64 us (2%)
    pallas_call x1, Pallas kernels, shards(): pl.pallas_call(functools.partial(kernel, g_size, b_size), out_shape=(jax....  29.7 us
    pallas_call x1, Pallas kernels, shards(): pl.pallas_call(hand_over, out_shape=tuple((jax.ShapeDtypeStruct(x.shape,...  11.1 us

profile of v2, /device:TPU:17, one launch (start us, length us, event | category | flops | bytes accessed | tf_op | source)
XLA Modules:
  0.0 41.4 jit_solution(825206888288399114)
XLA Ops:
  0.6 29.7 %basis_currents.1 = (f32[2,32,512]{2,1,0:T(8,128)}, f32[2,4,32,32]{3,2,1,0:T(8,128)}, f32[2,32,256]{2,1,0:T(8,128)}) custom-call(bf16[2,1024,256]{2,1,0:T(8,128)(2,1)} %ex.1, bf16[2,512,1024]{2,1,0:T(8,128)(2,1)} %inv.1, bf16[2,4,512,1024]{3,2,1,0:T(8,128)(2,1)} %coup.1, s32[2,4]{1,0:T(2,128)} %mask.1, f32[5,32,256]{2,1,0:T(8,128)} %bitcast.2), custom_call_target="tpu_custom_call" | custom-call | flops 2147483648 | bytes 10485760 | tf_op jit(solution)/shard_map/basis_currents/pallas_call | solution.py:458
  30.3 11.1 %hand_over.1 = (f32[2,32,512]{2,1,0:T(8,128)}, f32[2,4,32,32]{3,2,1,0:T(8,128)}, f32[2,32,256]{2,1,0:T(8,128)}) custom-call(f32[2,32,512]{2,1,0:T(8,128)} %get-tuple-element.9.a, f32[2,4,32,32]{3,2,1,0:T(8,128)} %get-tuple-element.10.b, f32[2,32,256]{2,1,0:T(8,128)} %get-tuple-element.11.c), custom_call_target="tpu_custom_call" | custom-call | tf_op jit(solution)/shard_map/hand_over/pallas_call | solution.py:513

commit v3 on v2

--- a/solution.py
+++ b/solution.py
@@ -82,11 +82,21 @@
     eye = (row == col).astype(F32)
     down = lax.broadcasted_iota(jnp.int32, (size, 1), 0)
     work = [jnp.concatenate([gram, eye], axis=1) for gram in grams]
-    for k in range(size - 1):
+    width = math.gcd(size, 8)
+    for first in range(0, size, width):
+        span = range(first, first + width)
         for n, a in enumerate(work):
-            line = a[k : k + 1, :] / a[k : k + 1, k : k + 1]
-            lead = jnp.where(down > k, a[:, k : k + 1], 0.0)
-            work[n] = a - lead * line
+            columns = {k: jnp.broadcast_to(a[:, k : k + 1], a.shape) for k in span}
+            lines = {k: a[k : k + 1, :] for k in span}
+            for k in span:
+                factor = 1.0 / columns[k][k : k + 1, :]
+                line = lines[k] * factor
+                lead = jnp.where(down > k, columns[k], 0.0)
+                for t in range(k + 1, first + width):
+                    lines[t] = lines[t] - columns[k][t : t + 1, :] * line
+                    columns[t] = columns[t] - lead * (columns[t][k : k + 1, :] * factor)
+                a = a - lead * line
+            work[n] = a
     out = []
     for a in work:
         diag = jnp.sum(jnp.where(row == col, a[:, :size], 0.0), axis=1, keepdims=True)
@@ -119,8 +129,9 @@
     for number, place in enumerate((7, 6, 0, 4, 2, 3, 1, 5)):
         i, k = USE[place]
         loads["c", i, k] = load(1 + 2 * blocks + number, coup.at[i, k], c_v.at[i, k])
-    for copy in loads.values():
-        copy.start()
+    for name, copy in loads.items():
+        if name[0] != "c":
+            copy.start()
 
     barrier = pltpu.get_barrier_semaphore()
 
@@ -192,6 +203,10 @@
     for i in range(blocks):
         loads["inv", i].wait()
         loads["ex", i].wait()
+        if i == blocks - 1:
+            for name, copy in loads.items():
+                if name[0] == "c":
+                    copy.start()
         primary = nn(inv_v[i], ex_v[i])
         primary_hi, primary_lo = terms(primary, 2)
         out_v[i] = folded(nt(flat_both, primary_hi), 2) + nt(flat_hi, primary_lo)
@@ -313,8 +328,6 @@
         project(0, k)
     send_projected(0)
     sketch_block(1)
-    for k in range(2):
-        project(1, k)
 
     for i in range(blocks):
         for copy in skp_copies[i]:
@@ -327,9 +340,8 @@
             got = exact_nt(part, part, 3)
             total = got if total is None else total + got
         grams.append(total * (1.0 / unknowns))
-    for k in range(2, slots):
+    for k in range(slots):
         project(1, k)
-    send_projected(1)
     inverses = inverse_factors(grams)
     for i in range(blocks):
         lin[i * r : (i + 1) * r, :] = jnp.concatenate([inverses[i]] * slots, axis=1)
@@ -339,20 +351,7 @@
         lin_copies.append((direction, copy))
         pl.when(sends(direction))(copy.start)
 
-    scale = 1.0 / math.sqrt(unknowns)
-    for i in range(blocks):
-        bases_v[i] = exact_nn(inverses[i], skt[g, i * r : (i + 1) * r, :], 3)
-        driven = None
-        for p in range(g_size):
-            got = nn(stacked(skt[p, i * r : (i + 1) * r, :], 3), ex_v[i, p * rows : (p + 1) * rows, :])
-            driven = got if driven is None else driven + got
-        re_v[i] = exact_nn(inverses[i], folded(driven, 3), 3) * scale
-    stores = [
-        pltpu.make_async_copy(bases_v, bases_o, store_sem.at[0]),
-        pltpu.make_async_copy(re_v, re_o, store_sem.at[1]),
-    ]
-    for copy in stores:
-        copy.start()
+    send_projected(1)
 
     wide = slots * r
     row = lax.broadcasted_iota(jnp.int32, (wide, wide), 0) // r
@@ -388,30 +387,44 @@
         direction, copy = sk_copies[side, i]
         pl.when(there(direction))(copy.wait_recv)
         reduce(users, near[side, i * r : (i + 1) * r, :])
-    for direction, copy in lin_copies:
-        pl.when(there(direction))(copy.wait_recv)
-
-    left_a, left_b = lin_near[0, 0:r, :], lin_near[0, r : 2 * r, :]
-    right_a, right_b = lin_near[1, 0:r, :], lin_near[1, r : 2 * r, :]
-    own_a, own_b = lin[0:r, :], lin[r : 2 * r, :]
-    beside = ((left_a, left_b, own_b, right_a), (left_b, own_a, right_a, right_b))
-    for i in range(blocks):
-        product = jnp.concatenate([products[i, k] for k in range(slots)], axis=1)
-        factors = jnp.where(diagonal, jnp.concatenate(beside[i], axis=0), 0.0)
-        wbuf[g, i * r : (i + 1) * r, :] = exact_nt(product, factors, 3)
+    for i in range(blocks):
+        wbuf[g, i * r : (i + 1) * r, :] = jnp.concatenate([products[i, k] for k in range(slots)], axis=1)
     here = wbuf.at[g]
     w_copies = to_peers(here, here, w_send, w_recv)
     for copy in w_copies:
         copy.start()
+
+    scale = 1.0 / math.sqrt(unknowns)
+    for i in range(blocks):
+        bases_v[i] = exact_nn(inverses[i], skt[g, i * r : (i + 1) * r, :], 3)
+        driven = None
+        for p in range(g_size):
+            got = nn(stacked(skt[p, i * r : (i + 1) * r, :], 3), ex_v[i, p * rows : (p + 1) * rows, :])
+            driven = got if driven is None else driven + got
+        re_v[i] = exact_nn(inverses[i], folded(driven, 3), 3) * scale
+    stores = [
+        pltpu.make_async_copy(bases_v, bases_o, store_sem.at[0]),
+        pltpu.make_async_copy(re_v, re_o, store_sem.at[1]),
+    ]
+    for copy in stores:
+        copy.start()
+
+    for direction, copy in lin_copies:
+        pl.when(there(direction))(copy.wait_recv)
     for copy in w_copies:
         copy.wait_recv()
     total = wbuf[0]
     for p in range(1, g_size):
         total = total + wbuf[p]
-    total = total * scale
-    for i in range(blocks):
+    left_a, left_b = lin_near[0, 0:r, :], lin_near[0, r : 2 * r, :]
+    right_a, right_b = lin_near[1, 0:r, :], lin_near[1, r : 2 * r, :]
+    own_a, own_b = lin[0:r, :], lin[r : 2 * r, :]
+    beside = ((left_a, left_b, own_b, right_a), (left_b, own_a, right_a, right_b))
+    for i in range(blocks):
+        factors = jnp.where(diagonal, jnp.concatenate(beside[i], axis=0), 0.0)
+        got = exact_nt(total[i * r : (i + 1) * r], factors, 3) * scale
         for k in range(slots):
-            rc_v[i, k] = total[i * r : (i + 1) * r, k * r : (k + 1) * r]
+            rc_v[i, k] = got[:, k * r : (k + 1) * r]
     last = pltpu.make_async_copy(rc_v, rc_o, store_sem.at[2])
     last.start()
 
@@ -429,17 +442,6 @@
     for copy in stores:
         copy.wait()
     last.wait()
-
-
-def hand_over(a, b, c, a_out, b_out, c_out, sems):
-    copies = [
-        pltpu.make_async_copy(source, target, sems.at[n])
-        for n, (source, target) in enumerate(((a, a_out), (b, b_out), (c, c_out)))
-    ]
-    for copy in copies:
-        copy.start()
-    for copy in copies:
-        copy.wait()
 
 
 def shards(g_size, b_size, excitation, inverse_self, coupling, neighbour_mask, sketch):
@@ -509,16 +511,6 @@
         ),
         name="basis_currents",
     )(excitation, inverse_self, coupling, neighbour_mask, sketch)
-    results = (bases, reduced, driven)
-    bases, reduced, driven = pl.pallas_call(
-        hand_over,
-        out_shape=tuple(jax.ShapeDtypeStruct(x.shape, x.dtype) for x in results),
-        in_specs=[anywhere] * 3,
-        out_specs=(anywhere,) * 3,
-        scratch_shapes=[dma(3)],
-        compiler_params=pltpu.CompilerParams(vmem_limit_bytes=60 * 1024 * 1024),
-        name="hand_over",
-    )(*results)
     return jnp.swapaxes(bases, 1, 2), reduced, driven
 
 

time: 41.5 us -> 33 us (0.80)
  Pallas kernels: 40.7 us -> 27.5 us
  local copies, waits for them, and re-layouts: 0 us -> 4.61 us
    pallas_call x1 -> x0, Pallas kernels: 11.1 us -> none  [shards(): pl.pallas_call(hand_over, out_shape=tuple((jax.ShapeDtypeStruct(x.shape,...]
    unnamed x0 -> x3, local copies, waits for them, and re-layouts: none -> 4.61 us
    pallas_call x1, Pallas kernels: 29.7 us -> 27.5 us  [shards(): pl.pallas_call(functools.partial(kernel, g_size, b_size), out_shape=(jax....]
where the time goes in v3:
time: 33 us; the launch traced here: 32.8 us
  Pallas kernels  27.5 us (83%)
  local copies, waits for them, and re-layouts  4.61 us (14%)
  between operations  0.64 us (2%)
    pallas_call x1, Pallas kernels, shards(): pl.pallas_call(functools.partial(kernel, g_size, b_size), out_shape=(jax....  27.5 us
    unnamed x3, local copies, waits for them, and re-layouts  4.61 us

profile of v3, /device:TPU:17, one launch (start us, length us, event | category | flops | bytes accessed | tf_op | source)
XLA Modules:
  0.0 32.8 jit_solution(12373998616090864487)
XLA Ops:
  0.6 27.5 %basis_currents.1 = (f32[2,32,512]{2,1,0:T(8,128)}, f32[2,4,32,32]{3,2,1,0:T(8,128)}, f32[2,32,256]{2,1,0:T(8,128)}) custom-call(bf16[2,1024,256]{2,1,0:T(8,128)(2,1)} %ex.1, bf16[2,512,1024]{2,1,0:T(8,128)(2,1)} %inv.1, bf16[2,4,512,1024]{3,2,1,0:T(8,128)(2,1)} %coup.1, s32[2,4]{1,0:T(2,128)} %mask.1, f32[5,32,256]{2,1,0:T(8,128)} %bitcast.2), custom_call_target="tpu_custom_call" | custom-call | flops 2147483648 | bytes 10485760 | tf_op jit(solution)/shard_map/basis_currents/pallas_call | solution.py:460
  28.1 1.6 %copy.11 = f32[2,512,32]{1,2,0:T(8,128)} copy(f32[2,512,32]{1,2,0:T(8,128)} %bitcast.3) | data formatting | bytes 262144
  29.7 1.6 %copy.12 = f32[2,4,32,32]{3,2,1,0:T(8,128)} copy(f32[2,4,32,32]{3,2,1,0:T(8,128)} %get-tuple-element.13) | data formatting | bytes 65536
  31.3 1.5 %copy.13 = f32[2,32,256]{2,1,0:T(8,128)} copy(f32[2,32,256]{2,1,0:T(8,128)} %get-tuple-element.14) | data formatting | bytes 131072

commit v4 on v3

--- a/solution.py
+++ b/solution.py
@@ -17,10 +17,8 @@
     (0, 1, 0, 6),
     (1, 1, 1, 2),
     (1, 2, 0, 7),
-    (0, 2, -1, 3),
-    (1, 0, 1, 1),
-    (1, 3, -1, 5),
 )
+LATER = (((0, 2, -1, 3), 4), ((1, 0, 1, 1), 0), ((1, 3, -1, 5), 2))
 USE = {0: (0, 0), 1: (1, 0), 2: (0, 1), 3: (1, 2), 4: (0, 3), 5: (1, 3), 6: (1, 1), 7: (0, 2)}
 
 
@@ -106,8 +104,8 @@
 
 def kernel(
     g_size, b_size, ex, inv, coup, mask, sketch, bases_o, rc_o, re_o,
-    ex_v, inv_v, c_v, sk_v, out_v, buf, src, skt, near, lin, lin_near, wbuf, v_out, v_in, bases_v, rc_v, re_v,
-    load_sem, store_sem, p1_send, p1_recv, p1_fsend, p1_frecv, src_send, src_recv,
+    ex_v, inv_v, c_v, sk_v, out_v, buf, src, skt, near, lin, lin_near, wbuf, v_out, v_in, mask_s,
+    load_sem, p1_send, p1_recv, p1_fsend, p1_frecv, src_send, src_recv,
     sk_send, sk_recv, skp_send, skp_recv, v_send, v_recv, lin_send, lin_recv, w_send, w_recv,
 ):
     b, g = lax.axis_index("blk"), lax.axis_index("grp")
@@ -123,6 +121,7 @@
 
     loads = {}
     loads["sketch"] = load(0, sketch, sk_v)
+    loads["mask"] = load(1 + 2 * blocks + blocks * slots, mask, mask_s)
     for i in range(blocks):
         loads["inv", i] = load(1 + 2 * i, inv.at[i], inv_v.at[i])
         loads["ex", i] = load(2 + 2 * i, ex.at[i], ex_v.at[i])
@@ -223,7 +222,8 @@
             total = got if total is None else total + got
         return folded(total, 3)
 
-    weights = [[mask[i, k].astype(F32) for k in range(slots)] for i in range(blocks)]
+    loads["mask"].wait()
+    weights = [[mask_s[i, k].astype(F32) for k in range(slots)] for i in range(blocks)]
     sources = [None] * blocks
 
     def add_source(place):
@@ -305,6 +305,10 @@
     for place in (7, 6):
         arrived(place)
         add_source(place)
+    for piece, first in LATER:
+        direction, copy = piece_copies[first]
+        pl.when(sends(direction))(copy.wait_send)
+        send_piece(*piece)
     forward((0, 4))
     arrived(0)
     add_source(0)
@@ -396,19 +400,12 @@
 
     scale = 1.0 / math.sqrt(unknowns)
     for i in range(blocks):
-        bases_v[i] = exact_nn(inverses[i], skt[g, i * r : (i + 1) * r, :], 3)
+        bases_o[i] = exact_nn(inverses[i], skt[g, i * r : (i + 1) * r, :], 3)
         driven = None
         for p in range(g_size):
             got = nn(stacked(skt[p, i * r : (i + 1) * r, :], 3), ex_v[i, p * rows : (p + 1) * rows, :])
             driven = got if driven is None else driven + got
-        re_v[i] = exact_nn(inverses[i], folded(driven, 3), 3) * scale
-    stores = [
-        pltpu.make_async_copy(bases_v, bases_o, store_sem.at[0]),
-        pltpu.make_async_copy(re_v, re_o, store_sem.at[1]),
-    ]
-    for copy in stores:
-        copy.start()
-
+        re_o[i] = exact_nn(inverses[i], folded(driven, 3), 3) * scale
     for direction, copy in lin_copies:
         pl.when(there(direction))(copy.wait_recv)
     for copy in w_copies:
@@ -424,11 +421,11 @@
         factors = jnp.where(diagonal, jnp.concatenate(beside[i], axis=0), 0.0)
         got = exact_nt(total[i * r : (i + 1) * r], factors, 3) * scale
         for k in range(slots):
-            rc_v[i, k] = got[:, k * r : (k + 1) * r]
-    last = pltpu.make_async_copy(rc_v, rc_o, store_sem.at[2])
-    last.start()
-
-    for direction, copy in list(piece_copies.values()) + list(sk_copies.values()) + lin_copies:
+            rc_o[i, k] = got[:, k * r : (k + 1) * r]
+
+    waited = [first for _, first in LATER]
+    last_pieces = [pair for place, pair in piece_copies.items() if place not in waited]
+    for direction, copy in last_pieces + list(sk_copies.values()) + lin_copies:
         pl.when(sends(direction))(copy.wait_send)
     for place, copies in own_copies.items():
         for copy in copies:
@@ -439,9 +436,6 @@
     for copies in list(src_copies.values()) + list(skp_copies.values()) + list(v_copies.values()) + [w_copies]:
         for copy in copies:
             copy.wait_send()
-    for copy in stores:
-        copy.wait()
-    last.wait()
 
 
 def shards(g_size, b_size, excitation, inverse_self, coupling, neighbour_mask, sketch):
@@ -459,13 +453,9 @@
     flops = 2 * blocks * rows * unknowns * (columns + 2 * slots * 3 * r)
     bases, reduced, driven = pl.pallas_call(
         functools.partial(kernel, g_size, b_size),
-        out_shape=(
-            jax.ShapeDtypeStruct((blocks, r, rows), F32),
-            jax.ShapeDtypeStruct((blocks, slots, r, r), F32),
-            jax.ShapeDtypeStruct((blocks, r, columns), F32),
-        ),
-        in_specs=[anywhere, anywhere, anywhere, pl.BlockSpec(memory_space=pltpu.SMEM), anywhere],
-        out_specs=(anywhere, anywhere, anywhere),
+        out_shape=(vmem(blocks, r, rows), vmem(blocks, slots, r, r), vmem(blocks, r, columns)),
+        in_specs=[anywhere] * 5,
+        out_specs=(pl.BlockSpec(memory_space=pltpu.VMEM),) * 3,
         scratch_shapes=[
             pltpu.VMEM(excitation.shape, BF16),
             pltpu.VMEM(inverse_self.shape, BF16),
@@ -481,11 +471,8 @@
             vmem(g_size, 2 * r, wide),
             vmem(g_size, blocks * wide, rows),
             vmem(others, blocks * wide, rows),
-            vmem(blocks, r, rows),
-            vmem(blocks, slots, r, r),
-            vmem(blocks, r, columns),
-            dma(1 + 2 * blocks + blocks * slots),
-            dma(3),
+            pltpu.SMEM(neighbour_mask.shape, neighbour_mask.dtype),
+            dma(2 + 2 * blocks + blocks * slots),
             dma(6),
             dma(6),
             dma(8, others),

time: 33 us -> 28.6 us (0.87)
  local copies, waits for them, and re-layouts: 4.61 us -> 1.94 us
  Pallas kernels: 27.5 us -> 25.9 us
    unnamed x3, local copies, waits for them, and re-layouts: 4.61 us -> 1.94 us
    pallas_call x1, Pallas kernels: 27.5 us -> 25.9 us  [shards(): pl.pallas_call(functools.partial(kernel, g_size, b_size), out_shape=(vmem...]
where the time goes in v4:
time: 28.6 us; the launch traced here: 28.5 us
  Pallas kernels  25.9 us (91%)
  local copies, waits for them, and re-layouts  1.94 us (7%)
  between operations  0.64 us (2%)
    pallas_call x1, Pallas kernels, shards(): pl.pallas_call(functools.partial(kernel, g_size, b_size), out_shape=(vmem...  25.9 us
    unnamed x3, local copies, waits for them, and re-layouts  1.94 us

profile of v4, /device:TPU:17, one launch (start us, length us, event | category | flops | bytes accessed | tf_op | source)
XLA Modules:
  0.0 28.5 jit_solution(4707167067346220261)
XLA Ops:
  0.6 25.9 %basis_currents.1 = (f32[2,32,512]{2,1,0:T(8,128)S(1)}, f32[2,4,32,32]{3,2,1,0:T(8,128)S(1)}, f32[2,32,256]{2,1,0:T(8,128)S(1)}) custom-call(bf16[2,1024,256]{2,1,0:T(8,128)(2,1)} %ex.1, bf16[2,512,1024]{2,1,0:T(8,128)(2,1)} %inv.1, bf16[2,4,512,1024]{3,2,1,0:T(8,128)(2,1)} %coup.1, s32[2,4]{1,0:T(2,128)} %mask.1, f32[5,32,256]{2,1,0:T(8,128)} %bitcast.3), custom_call_target="tpu_custom_call" | custom-call | flops 2147483648 | bytes 10485760 | tf_op jit(solution)/shard_map/basis_currents/pallas_call | solution.py:454
  26.5 0.7 %copy.11 = f32[2,512,32]{1,2,0:T(8,128)} copy(f32[2,512,32]{1,2,0:T(8,128)S(1)} %bitcast.2) | data formatting | bytes 262144
  27.2 0.6 %copy.13 = f32[2,32,256]{2,1,0:T(8,128)} copy(f32[2,32,256]{2,1,0:T(8,128)S(1)} %get-tuple-element.11) | data formatting | bytes 131072
  27.8 0.7 %copy.12 = f32[2,4,32,32]{3,2,1,0:T(8,128)} copy(f32[2,4,32,32]{3,2,1,0:T(8,128)S(1)} %get-tuple-element.10) | data formatting | bytes 65536

commit v5 on v4

--- a/solution.py
+++ b/solution.py
@@ -215,22 +215,25 @@
         for piece in PIECES[:3] if i == 0 else PIECES[3:]:
             send_piece(*piece)
 
-    def coupled(i, k, parts):
-        total = None
-        for p in range(g_size):
-            got = nt(stacked(parts[p], 3), c_v[i, k, :, p * rows : (p + 1) * rows])
-            total = got if total is None else total + got
-        return folded(total, 3)
-
     loads["mask"].wait()
     weights = [[mask_s[i, k].astype(F32) for k in range(slots)] for i in range(blocks)]
     sources = [None] * blocks
 
-    def add_source(place):
+    def add_part(place, p):
         i, k = USE[place]
-        loads["c", i, k].wait()
-        term = weights[i][k] * coupled(i, k, [buf[p, place * r : (place + 1) * r, :] for p in range(g_size)])
+        piece = stacked(buf[p, place * r : (place + 1) * r, :], 3)
+        columns = pl.ds(pl.multiple_of(p * rows, rows), rows)
+        term = weights[i][k] * folded(nt(piece, c_v[i, k, :, columns]), 3)
         sources[i] = term if sources[i] is None else sources[i] + term
+
+    def add_own(place):
+        loads["c", *USE[place]].wait()
+        add_part(place, g)
+
+    def add_others(place):
+        arrived(place)
+        for peer in peers:
+            add_part(place, peer)
 
     def forward(places):
         for place in places:
@@ -303,35 +306,35 @@
             copy.start()
 
     for place in (7, 6):
-        arrived(place)
-        add_source(place)
+        add_own(place)
+    for place in (7, 6):
+        add_others(place)
     for piece, first in LATER:
         direction, copy = piece_copies[first]
         pl.when(sends(direction))(copy.wait_send)
         send_piece(*piece)
-    forward((0, 4))
-    arrived(0)
-    add_source(0)
-    forward((2,))
-    arrived(4)
-    add_source(4)
-    arrived(2)
-    add_source(2)
+    for place in (0, 4, 2):
+        forward((place,))
+        add_own(place)
+    for place in (0, 4, 2):
+        add_others(place)
     finish_source(0)
     forward((3,))
+    add_own(3)
     sketch_block(0)
-    forward((1, 5))
-    arrived(3)
-    add_source(3)
-    arrived(1)
-    add_source(1)
-    arrived(5)
-    add_source(5)
+    for place in (1, 5):
+        forward((place,))
+        add_own(place)
+    for place in (3, 1, 5):
+        add_others(place)
     finish_source(1)
-    for k in range(slots):
+    for k in range(2):
+        project(0, k)
+    sketch_block(1)
+    for k in range(2, slots):
         project(0, k)
     send_projected(0)
-    sketch_block(1)
+    project(1, 0)
 
     for i in range(blocks):
         for copy in skp_copies[i]:
@@ -344,11 +347,13 @@
             got = exact_nt(part, part, 3)
             total = got if total is None else total + got
         grams.append(total * (1.0 / unknowns))
-    for k in range(slots):
+    for k in range(1, slots):
         project(1, k)
     inverses = inverse_factors(grams)
-    for i in range(blocks):
-        lin[i * r : (i + 1) * r, :] = jnp.concatenate([inverses[i]] * slots, axis=1)
+    half = r // 2
+    lin[...] = jnp.concatenate(
+        [inverse[n : n + half] for inverse in inverses for n in (0, half)], axis=1
+    )
     lin_copies = []
     for side, direction in enumerate((1, -1)):
         copy = remote(lin, lin_near.at[side], lin_send.at[side], lin_recv.at[side], (b + direction, g))
@@ -361,6 +366,16 @@
     row = lax.broadcasted_iota(jnp.int32, (wide, wide), 0) // r
     col = lax.broadcasted_iota(jnp.int32, (wide, wide), 1) // r
     diagonal = row == col
+
+    def wider(x):
+        return jnp.concatenate([x] * slots, axis=1)
+
+    def unpacked(x):
+        quarters = [x[:, n * r : (n + 1) * r] for n in range(2 * blocks)]
+        return [
+            wider(jnp.concatenate(quarters[2 * i : 2 * i + 2], axis=0)) for i in range(blocks)
+        ]
+
     projected = []
     for i in range(blocks):
         for copy in v_copies[i]:
@@ -369,7 +384,7 @@
         total = v_out[g, pl.ds(i * wide, wide), :]
         for d in range(g_size - 1):
             total = total + v_in[d, span, :]
-        factors = jnp.where(diagonal, jnp.concatenate([lin[i * r : (i + 1) * r, :]] * slots, axis=0), 0.0)
+        factors = jnp.where(diagonal, jnp.concatenate([wider(inverses[i])] * slots, axis=0), 0.0)
         projected.append(exact_nn(factors, total, 3))
 
     products = {}
@@ -413,9 +428,8 @@
     total = wbuf[0]
     for p in range(1, g_size):
         total = total + wbuf[p]
-    left_a, left_b = lin_near[0, 0:r, :], lin_near[0, r : 2 * r, :]
-    right_a, right_b = lin_near[1, 0:r, :], lin_near[1, r : 2 * r, :]
-    own_a, own_b = lin[0:r, :], lin[r : 2 * r, :]
+    (left_a, left_b), (right_a, right_b) = unpacked(lin_near[0]), unpacked(lin_near[1])
+    own_a, own_b = [wider(inverse) for inverse in inverses]
     beside = ((left_a, left_b, own_b, right_a), (left_b, own_a, right_a, right_b))
     for i in range(blocks):
         factors = jnp.where(diagonal, jnp.concatenate(beside[i], axis=0), 0.0)
@@ -466,8 +480,8 @@
             vmem(g_size, 2 * r, rows),
             vmem(g_size, 2 * r, rows),
             vmem(2, 2 * r, rows),
-            vmem(2 * r, wide),
-            vmem(2, 2 * r, wide),
+            vmem(r // 2, 2 * blocks * r),
+            vmem(2, r // 2, 2 * blocks * r),
             vmem(g_size, 2 * r, wide),
             vmem(g_size, blocks * wide, rows),
             vmem(others, blocks * wide, rows),

time: 28.6 us -> 28.3 us (0.990)
  Pallas kernels: 25.9 us -> 25.6 us
    pallas_call x1, Pallas kernels: 25.9 us -> 25.6 us  [shards(): pl.pallas_call(functools.partial(kernel, g_size, b_size), out_shape=(vmem...]
where the time goes in v5:
time: 28.3 us; the launch traced here: 28.2 us
  Pallas kernels  25.6 us (90%)
  local copies, waits for them, and re-layouts  1.94 us (7%)
  between operations  0.64 us (2%)
    pallas_call x1, Pallas kernels, shards(): pl.pallas_call(functools.partial(kernel, g_size, b_size), out_shape=(vmem...  25.6 us
    unnamed x3, local copies, waits for them, and re-layouts  1.94 us

profile of v5, /device:TPU:17, one launch (start us, length us, event | category | flops | bytes accessed | tf_op | source)
XLA Modules:
  0.0 28.2 jit_solution(18075837124892422053)
XLA Ops:
  0.6 25.6 %basis_currents.1 = (f32[2,32,512]{2,1,0:T(8,128)S(1)}, f32[2,4,32,32]{3,2,1,0:T(8,128)S(1)}, f32[2,32,256]{2,1,0:T(8,128)S(1)}) custom-call(bf16[2,1024,256]{2,1,0:T(8,128)(2,1)} %ex.1, bf16[2,512,1024]{2,1,0:T(8,128)(2,1)} %inv.1, bf16[2,4,512,1024]{3,2,1,0:T(8,128)(2,1)} %coup.1, s32[2,4]{1,0:T(2,128)} %mask.1, f32[5,32,256]{2,1,0:T(8,128)} %bitcast.3), custom_call_target="tpu_custom_call" | custom-call | flops 2147483648 | bytes 10485760 | tf_op jit(solution)/shard_map/basis_currents/pallas_call | solution.py:468
  26.2 0.7 %copy.11 = f32[2,512,32]{1,2,0:T(8,128)} copy(f32[2,512,32]{1,2,0:T(8,128)S(1)} %bitcast.2) | data formatting | bytes 262144
  26.9 0.6 %copy.13 = f32[2,32,256]{2,1,0:T(8,128)} copy(f32[2,32,256]{2,1,0:T(8,128)S(1)} %get-tuple-element.11) | data formatting | bytes 131072
  27.5 0.7 %copy.12 = f32[2,4,32,32]{3,2,1,0:T(8,128)} copy(f32[2,4,32,32]{3,2,1,0:T(8,128)S(1)} %get-tuple-element.10) | data formatting | bytes 65536

commit v6 on v5

--- a/solution.py
+++ b/solution.py
@@ -322,19 +322,21 @@
     forward((3,))
     add_own(3)
     sketch_block(0)
+    for k in range(2):
+        project(0, k)
     for place in (1, 5):
         forward((place,))
         add_own(place)
     for place in (3, 1, 5):
         add_others(place)
     finish_source(1)
-    for k in range(2):
-        project(0, k)
-    sketch_block(1)
     for k in range(2, slots):
         project(0, k)
     send_projected(0)
-    project(1, 0)
+    sketch_block(1)
+    for k in range(slots):
+        project(1, k)
+    send_projected(1)
 
     for i in range(blocks):
         for copy in skp_copies[i]:
@@ -347,8 +349,6 @@
             got = exact_nt(part, part, 3)
             total = got if total is None else total + got
         grams.append(total * (1.0 / unknowns))
-    for k in range(1, slots):
-        project(1, k)
     inverses = inverse_factors(grams)
     half = r // 2
     lin[...] = jnp.concatenate(
@@ -359,8 +359,6 @@
         copy = remote(lin, lin_near.at[side], lin_send.at[side], lin_recv.at[side], (b + direction, g))
         lin_copies.append((direction, copy))
         pl.when(sends(direction))(copy.start)
-
-    send_projected(1)
 
     wide = slots * r
     row = lax.broadcasted_iota(jnp.int32, (wide, wide), 0) // r
@@ -450,6 +448,17 @@
     for copies in list(src_copies.values()) + list(skp_copies.values()) + list(v_copies.values()) + [w_copies]:
         for copy in copies:
             copy.wait_send()
+
+
+def hand_over(a, b, c, a_out, b_out, c_out, sems):
+    copies = [
+        pltpu.make_async_copy(source, target, sems.at[n])
+        for n, (source, target) in enumerate(((a, a_out), (b, b_out), (c, c_out)))
+    ]
+    for copy in copies:
+        copy.start()
+    for copy in copies:
+        copy.wait()
 
 
 def shards(g_size, b_size, excitation, inverse_self, coupling, neighbour_mask, sketch):
@@ -512,6 +521,15 @@
         ),
         name="basis_currents",
     )(excitation, inverse_self, coupling, neighbour_mask, sketch)
+    results = (bases, reduced, driven)
+    bases, reduced, driven = pl.pallas_call(
+        hand_over,
+        out_shape=tuple(jax.ShapeDtypeStruct(x.shape, x.dtype) for x in results),
+        in_specs=[pl.BlockSpec(memory_space=pltpu.VMEM)] * 3,
+        out_specs=(anywhere,) * 3,
+        scratch_shapes=[dma(3)],
+        name="hand_over",
+    )(*results)
     return jnp.swapaxes(bases, 1, 2), reduced, driven
 
 

time: 28.3 us -> 30.4 us (1.074)
  Pallas kernels: 25.6 us -> 27.7 us
    pallas_call x0 -> x1, Pallas kernels: none -> 1.71 us  [shards(): pl.pallas_call(hand_over, out_shape=tuple((jax.ShapeDtypeStruct(x.shape,...]
    pallas_call x1, Pallas kernels: 25.6 us -> 26 us  [shards(): pl.pallas_call(functools.partial(kernel, g_size, b_size), out_shape=(vmem...]
    unnamed x3 -> x6, local copies, waits for them, and re-layouts: 1.94 us -> 1.9 us
where the time goes in v6:
time: 30.4 us; the launch traced here: 30.2 us
  Pallas kernels  27.7 us (91%)
  local copies, waits for them, and re-layouts  1.9 us (6%)
  between operations  0.65 us (2%)
    pallas_call x1, Pallas kernels, shards(): pl.pallas_call(functools.partial(kernel, g_size, b_size), out_shape=(vmem...  26 us
    unnamed x6, local copies, waits for them, and re-layouts  1.9 us
    pallas_call x1, Pallas kernels, shards(): pl.pallas_call(hand_over, out_shape=tuple((jax.ShapeDtypeStruct(x.shape,...  1.71 us

profile of v6, /device:TPU:17, one launch (start us, length us, event | category | flops | bytes accessed | tf_op | source)
XLA Modules:
  0.0 30.2 jit_solution(5292850227995349441)
XLA Ops:
  0.6 26.0 %basis_currents.1 = (f32[2,32,512]{2,1,0:T(8,128)S(1)}, f32[2,4,32,32]{3,2,1,0:T(8,128)S(1)}, f32[2,32,256]{2,1,0:T(8,128)S(1)}) custom-call(bf16[2,1024,256]{2,1,0:T(8,128)(2,1)} %ex.1, bf16[2,512,1024]{2,1,0:T(8,128)(2,1)} %inv.1, bf16[2,4,512,1024]{3,2,1,0:T(8,128)(2,1)} %coup.1, s32[2,4]{1,0:T(2,128)} %mask.1, f32[5,32,256]{2,1,0:T(8,128)} %bitcast.2), custom_call_target="tpu_custom_call" | custom-call | flops 2147483648 | bytes 10485760 | tf_op jit(solution)/shard_map/basis_currents/pallas_call | solution.py:477
  26.6 0.0 copy-start
  26.6 0.6 %copy-done = f32[2,32,512]{2,1,0:T(8,128)} copy-done((f32[2,32,512]{2,1,0:T(8,128)}, f32[2,32,512]{2,1,0:T(8,128)S(1)}, u32[]{:S(2)}) %copy-start) | copy-done | bytes 131096
  27.3 0.0 copy-start.1
  27.3 0.6 %copy-done.1 = f32[2,4,32,32]{3,2,1,0:T(8,128)} copy-done((f32[2,4,32,32]{3,2,1,0:T(8,128)}, f32[2,4,32,32]{3,2,1,0:T(8,128)S(1)}, u32[]{:S(2)}) %copy-start.1) | copy-done | bytes 32792
  27.9 0.0 copy-start.2
  27.9 0.6 %copy-done.2 = f32[2,32,256]{2,1,0:T(8,128)} copy-done((f32[2,32,256]{2,1,0:T(8,128)}, f32[2,32,256]{2,1,0:T(8,128)S(1)}, u32[]{:S(2)}) %copy-start.2) | copy-done | bytes 65560
  28.5 1.7 %hand_over.1 = (f32[2,32,512]{2,1,0:T(8,128)}, f32[2,4,32,32]{3,2,1,0:T(8,128)}, f32[2,32,256]{2,1,0:T(8,128)}) custom-call(f32[2,32,512]{2,1,0:T(8,128)} %copy-done, f32[2,4,32,32]{3,2,1,0:T(8,128)} %copy-done.1, f32[2,32,256]{2,1,0:T(8,128)} %copy-done.2), custom_call_target="tpu_custom_call" | custom-call | tf_op jit(solution)/shard_map/hand_over/pallas_call | solution.py:525
Async XLA Ops:
  26.6 0.7 %copy-start = (f32[2,32,512]{2,1,0:T(8,128)}, f32[2,32,512]{2,1,0:T(8,128)S(1)}, u32[]{:S(2)}) copy-start(f32[2,32,512]{2,1,0:T(8,128)S(1)} %get-tuple-element.9.a) | copy-start | bytes 393220
  27.3 0.6 %copy-start.1 = (f32[2,4,32,32]{3,2,1,0:T(8,128)}, f32[2,4,32,32]{3,2,1,0:T(8,128)S(1)}, u32[]{:S(2)}) copy-start(f32[2,4,32,32]{3,2,1,0:T(8,128)S(1)} %get-tuple-element.10.b) | copy-start | bytes 98308
  27.9 0.6 %copy-start.2 = (f32[2,32,256]{2,1,0:T(8,128)}, f32[2,32,256]{2,1,0:T(8,128)S(1)}, u32[]{:S(2)}) copy-start(f32[2,32,256]{2,1,0:T(8,128)S(1)} %get-tuple-element.11.c) | copy-start | bytes 196612

commit v7 on v5

--- a/solution.py
+++ b/solution.py
@@ -17,8 +17,10 @@
     (0, 1, 0, 6),
     (1, 1, 1, 2),
     (1, 2, 0, 7),
+    (0, 2, -1, 3),
+    (1, 0, 1, 1),
+    (1, 3, -1, 5),
 )
-LATER = (((0, 2, -1, 3), 4), ((1, 0, 1, 1), 0), ((1, 3, -1, 5), 2))
 USE = {0: (0, 0), 1: (1, 0), 2: (0, 1), 3: (1, 2), 4: (0, 3), 5: (1, 3), 6: (1, 1), 7: (0, 2)}
 
 
@@ -309,10 +311,6 @@
         add_own(place)
     for place in (7, 6):
         add_others(place)
-    for piece, first in LATER:
-        direction, copy = piece_copies[first]
-        pl.when(sends(direction))(copy.wait_send)
-        send_piece(*piece)
     for place in (0, 4, 2):
         forward((place,))
         add_own(place)
@@ -437,9 +435,7 @@
         for k in range(slots):
             rc_o[i, k] = got[:, k * r : (k + 1) * r]
 
-    waited = [first for _, first in LATER]
-    last_pieces = [pair for place, pair in piece_copies.items() if place not in waited]
-    for direction, copy in last_pieces + list(sk_copies.values()) + lin_copies:
+    for direction, copy in list(piece_copies.values()) + list(sk_copies.values()) + lin_copies:
         pl.when(sends(direction))(copy.wait_send)
     for place, copies in own_copies.items():
         for copy in copies:

time: 28.3 us -> 28.3 us (level)
  no operation moved by 1% of the time
where the time goes in v7:
time: 28.3 us; the launch traced here: 28.2 us
  Pallas kernels  25.6 us (90%)
  local copies, waits for them, and re-layouts  1.94 us (7%)
  between operations  0.64 us (2%)
    pallas_call x1, Pallas kernels, shards(): pl.pallas_call(functools.partial(kernel, g_size, b_size), out_shape=(vmem...  25.6 us
    unnamed x3, local copies, waits for them, and re-layouts  1.94 us

profile of v7, /device:TPU:17, one launch (start us, length us, event | category | flops | bytes accessed | tf_op | source)
XLA Modules:
  0.0 28.2 jit_solution(840947953510582478)
XLA Ops:
  0.6 25.6 %basis_currents.1 = (f32[2,32,512]{2,1,0:T(8,128)S(1)}, f32[2,4,32,32]{3,2,1,0:T(8,128)S(1)}, f32[2,32,256]{2,1,0:T(8,128)S(1)}) custom-call(bf16[2,1024,256]{2,1,0:T(8,128)(2,1)} %ex.1, bf16[2,512,1024]{2,1,0:T(8,128)(2,1)} %inv.1, bf16[2,4,512,1024]{3,2,1,0:T(8,128)(2,1)} %coup.1, s32[2,4]{1,0:T(2,128)} %mask.1, f32[5,32,256]{2,1,0:T(8,128)} %bitcast.3), custom_call_target="tpu_custom_call" | custom-call | flops 2147483648 | bytes 10485760 | tf_op jit(solution)/shard_map/basis_currents/pallas_call | solution.py:464
  26.2 0.7 %copy.11 = f32[2,512,32]{1,2,0:T(8,128)} copy(f32[2,512,32]{1,2,0:T(8,128)S(1)} %bitcast.2) | data formatting | bytes 262144
  26.9 0.6 %copy.13 = f32[2,32,256]{2,1,0:T(8,128)} copy(f32[2,32,256]{2,1,0:T(8,128)S(1)} %get-tuple-element.11) | data formatting | bytes 131072
  27.5 0.7 %copy.12 = f32[2,4,32,32]{3,2,1,0:T(8,128)} copy(f32[2,4,32,32]{3,2,1,0:T(8,128)S(1)} %get-tuple-element.10) | data formatting | bytes 65536
